TPU v7x, 512 devices: a whole 4x8x8 slice. The times are simulated.
512 devices in a mesh: rep: 32 (over x, z_lo, core), fsdp: 16 (over z_hi, y).
Axes of the slice: x: 4, y: 8, z: 8 (z_hi: 2, z_lo: 4; z = z_hi * 4 + z_lo), core: 2. Of those that a mesh axis runs over, the one named last changes fastest.
Arguments:
- local_params: bfloat16 [32, 256, 45056], P('rep', None, 'fsdp'), may hold values from -40 to 40
- base_params: bfloat16 [256, 45056], P(None, 'fsdp'), may hold values from -3 to 3
- momentum: float32 [256, 45056], P('rep', 'fsdp'), may hold values from -3 to 3
- encode_exponents: int32 [2, 352], P(None, 'fsdp'), may hold values from -9 to -5
- return_exponents: int32 [2, 352], P(None, 'fsdp'), may hold values from -12 to -8
Outputs:
- new_params: bfloat16 [256, 45056], P(None, 'fsdp')
- new_momentum: float32 [256, 45056], P('rep', 'fsdp')
All inputs are finite; a program needn't handle non-finite values.
Results may differ from a plain program's by a relative error of at most 0.0065.
Values may be sent and summed in bfloat16 or wider, within the bound.
A program may use at most 64 MiB of HBM per device.

v0:
```python
import jax
import jax.numpy as jnp
from jax import lax
from jax.sharding import PartitionSpec as P

BLOCK = 128


CODE_LIMIT = 448.0
MOMENTUM_RATE = 0.9
OUTER_RATE = 0.7


def expand(exponents):
    block_rows, block_cols = exponents.shape
    factor = jnp.exp2(exponents.astype(jnp.float32))
    spread = jnp.broadcast_to(factor[:, None, :, None], (block_rows, BLOCK, block_cols, BLOCK))
    return spread.reshape(block_rows * BLOCK, block_cols * BLOCK)


def sync_piece(params, base_piece, moment, enc_exp, ret_exp):
    scale_in = expand(enc_exp)
    scale_out = expand(ret_exp)
    base_wide = base_piece.astype(jnp.float32)
    encoded = jnp.clip(
        (params.astype(jnp.float32) - base_wide) / scale_in, -CODE_LIMIT, CODE_LIMIT
    ).astype(jnp.bfloat16)
    summed = lax.psum_scatter(encoded.astype(jnp.float32), "rep", scatter_dimension=0, tiled=True)
    owned_rows = summed.shape[0]
    first_row = lax.axis_index("rep") * owned_rows
    own_in = lax.dynamic_slice_in_dim(scale_in, first_row, owned_rows, 0)
    own_out = lax.dynamic_slice_in_dim(scale_out, first_row, owned_rows, 0)
    outer_grad = summed * own_in / lax.axis_size("rep")
    new_moment = MOMENTUM_RATE * moment + outer_grad
    outer_step = OUTER_RATE * (outer_grad + MOMENTUM_RATE * new_moment)
    delta_code = jnp.clip(outer_step / own_out, -CODE_LIMIT, CODE_LIMIT).astype(jnp.bfloat16)
    all_codes = lax.all_gather(delta_code, "rep", axis=0, tiled=True)
    updated = (base_wide + all_codes.astype(jnp.float32) * scale_out).astype(jnp.bfloat16)
    return (updated, new_moment)


def on_device(local_params, base_params, momentum, encode_exponents, return_exponents):
    params = local_params[0]
    updated, new_moment = sync_piece(
        params, base_params, momentum, encode_exponents, return_exponents
    )
    return (updated, new_moment)


def solution(mesh):
    return jax.shard_map(
        on_device,
        mesh=mesh,
        in_specs=(
            P("rep", None, "fsdp"),
            P(None, "fsdp"),
            P("rep", "fsdp"),
            P(None, "fsdp"),
            P(None, "fsdp"),
        ),
        out_specs=(P(None, "fsdp"), P("rep", "fsdp")),
        check_vma=False,
    )
```

profile of v0, /device:TPU:1, one launch (start us, length us, event | category | flops | bytes accessed | tf_op | source)
XLA Modules:
  0.0 253.8 jit_solution(340949191560853838)
XLA Ops:
  7.2 0.0 copy-start.2
  7.2 0.0 reduce-scatter.4.cloned.1.call-start
  7.2 0.8 multiply_exponential_fusion.1
  8.0 0.1 copy.27
  8.1 2.5 copy.25
  10.6 0.0 copy-done.2
  10.6 1.6 copy.26
  12.2 0.0 copy-start
  12.2 0.0 copy-start.1
  12.2 0.8 broadcast_in_dim.4
  13.0 0.5 copy-done
  13.6 0.4 copy-done.1
  14.0 2.2 fusion.4
  16.2 3.4 %copy.34 = f32[256,2816]{1,0:T(8,128)} copy(f32[256,2816]{0,1:T(8,128)} %fusion.4) | data formatting | bytes 5767168
  19.5 0.0 reduce-scatter.4.cloned.1.call-update
  19.6 0.0 all-gather.2.cloned.1.call-start
  19.6 0.0 copy-start.4
  19.6 1.8 copy.47
  21.5 0.0 copy-done.4
  21.5 0.1 copy.30
  21.6 0.8 broadcast_in_dim.5
  22.4 1.8 copy.46
  24.2 4.2 %constant_dynamic-slice_fusion = (f32[8,2816]{0,1:T(8,128)}, f32[8,2816]{0,1:T(8,128)}) fusion(f32[256,2816]{0,1:T(8,128)} %bitcast.27, s32[]{:T(128)S(6)} %select_n.4, f32[256,2816]{0,1:T(8,128)} %bitcast.26), kind=kLoop, calls=%fused_computation.14 | loop fusion | bytes 360452 | tf_op jit(solution)/shard_map/dynamic_slice | solution.py:32
  28.4 0.0 copy-start.3
  28.4 1.8 copy.37
  30.2 1.8 copy.36
  32.0 140.3 %reduce-scatter.4.cloned.1.call-done = f32[8,2816]{1,0:T(8,128)} async-done(((f32[256,2816]{1,0:T(8,128)}), f32[8,2816]{1,0:T(8,128)}) %reduce-scatter.4.cloned.1.call-update) | async-done | bytes 90128 | tf_op jit(solution)/shard_map/reduce_scatter | solution.py:28
  172.3 0.0 copy-done.3
  172.3 1.6 clamp_convert_fusion
  173.9 0.0 all-gather.2.cloned.1.call-update
  173.9 64.8 %all-gather.2.cloned.1.call-done = bf16[256,2816]{1,0:T(8,128)(2,1)} async-done(((bf16[8,2816]{1,0:T(8,128)(2,1)}), bf16[256,2816]{1,0:T(8,128)(2,1)}) %all-gather.2.cloned.1.call-update) | async-done | bytes 1441808 | tf_op jit(solution)/shard_map/all_gather | solution.py:37
  238.6 2.5 copy.32
  241.2 3.3 %fusion.3 = bf16[256,2816]{0,1:T(8,128)(2,1)} fusion(bf16[256,2816]{0,1:T(8,128)(2,1)} %copy.25, bf16[256,2816]{0,1:T(8,128)(2,1)} %copy.32, f32[352,8,2,128]{3,2,1,0:T(2,128)S(1)} %bitcast.23), kind=kLoop, calls=%fused_computation.5 | loop fusion | flops 3604480 | bytes 7208960 | tf_op jit(solution)/shard_map/convert_element_type | solution.py:38
  244.5 2.5 copy.33
  (1 shorter events, 0.0 us)
Async XLA Ops:
  7.2 3.5 %copy-start.2 = (bf16[1,256,2816]{2,1,0:T(8,128)(2,1)S(1)}, bf16[1,256,2816]{2,1,0:T(8,128)(2,1)}, u32[]{:S(2)}) copy-start(bf16[1,256,2816]{2,1,0:T(8,128)(2,1)} %param.5) | copy-start | bytes 4325380
  7.2 165.1 %reduce-scatter.4.cloned.1.call-start = ((), (), s32[]{:S(2)}) async-start(), calls=%async_computation.2 | async-start | bytes 2973696 | tf_op jit(solution)/shard_map/reduce_scatter | solution.py:28
  12.2 1.4 copy-start
  12.2 1.8 copy-start.1
  19.6 219.1 %all-gather.2.cloned.1.call-start = ((), (), s32[]{:S(2)}) async-start(), calls=%async_computation.1 | async-start | bytes 1486848 | tf_op jit(solution)/shard_map/all_gather | solution.py:37
  19.6 1.8 copy-start.4
  28.4 143.9 %copy-start.3 = (f32[8,2816]{1,0:T(8,128)S(1)}, f32[8,2816]{1,0:T(8,128)}, u32[]{:S(2)}) copy-start(f32[8,2816]{1,0:T(8,128)} %param.7) | copy-start | bytes 270340
Sparse Core Ops, SparseCore 0:
  19.7 152.5 reduce-scatter.3
  174.4 64.1 all-gather.1
where the time goes:
time: 254 us
  waiting for transfers between devices  205 us (81%)
  local copies, waits for them, and re-layouts  26.8 us (11%)
  between operations  14.1 us (6%)
  other arithmetic  7.84 us (3%)
    reduce_scatter x1, waiting for transfers between devices, sync_piece(): lax.psum_scatter(encoded.astype(jnp.float32), 'rep', scatter_dimension=0,...  140 us
    all_gather x1, waiting for transfers between devices, sync_piece(): all_codes = lax.all_gather(delta_code, 'rep', axis=0, tiled=True)  64.8 us
    unnamed x18, local copies, waits for them, and re-layouts  18.2 us
  transfers between devices with their start and end apart: 2, of which 2 were waited for; matrix products, arithmetic and copies ran while one was open for 5% of the time, Pallas kernels for 0%

commit v1 on v0

v1 whole, which is shorter than its diff:
```python
import functools

import jax
import jax.numpy as jnp
from jax import lax
from jax.experimental import pallas as pl
from jax.experimental.pallas import tpu as pltpu
from jax.sharding import PartitionSpec as P

BLOCK = 128
CODE_LIMIT = 448.0
MOMENTUM_RATE = 0.9
OUTER_RATE = 0.7
MESH = pl.DeviceIdType.MESH
NX, NZ = 4, 4
XROWS, ZROWS = 64, 16
HALF = XROWS // 2
CHUNKS = ((0, 4), (4, 8), (8, 11))
BF16, F32 = jnp.bfloat16, jnp.float32


def power_of_two(exponent):
    size = jnp.abs(exponent)
    result = jnp.ones(exponent.shape, F32)
    for bit in range(7):
        up, down = 2.0 ** (1 << bit) if bit < 7 else 1.0, 2.0 ** -(1 << bit)
        factor = jnp.where(exponent < 0, down, up)
        result = result * jnp.where((size & (1 << bit)) != 0, factor, 1.0)
    return result


def kernel(
    params, base, momentum, enc_exp, ret_exp, new_params, new_momentum,
    own_params, sib_params, own_base, oth_base, exps, enc_mul, enc_scale, ret_mul, ret_scale,
    s_far, s_right, s_left, f_up, f_dn, x_left, x_right, t_wide, t_narrow, z_in,
    moment, moment_out, moment_in, codes, sib_codes, own_out, oth_out,
    local_sem, send_sem, recv_sem,
):
    rep = lax.axis_index("rep")
    x, z, c = rep // (NZ * 2), (rep // 2) % NZ, rep % 2
    tiles = own_params.shape[1] // BLOCK
    width = tiles * BLOCK

    def place(px, pz, pc):
        return {"rep": (px * NZ + pz) * 2 + pc}

    sibling = place(x, z, 1 - c)
    right, left, far = (x + 1) % NX, (x + 3) % NX, (x + 2) % NX
    x_right_dev, x_left_dev = place(right, z, c), place(left, z, c)
    z_devs = [place(x, (z + d) % NZ, c) for d in (1, 2, 3)]

    def rows_of(block, first=0, count=XROWS):
        return pl.ds(pl.multiple_of(block * XROWS + first, 16), count)

    own_cols = pl.ds(pl.multiple_of(c * width, BLOCK), width)
    oth_cols = pl.ds(pl.multiple_of((1 - c) * width, BLOCK), width)

    counts = {"local": 0, "remote": 0}
    sends = []

    def local(src, dst):
        i = counts["local"]
        counts["local"] += 1
        copy = pltpu.make_async_copy(src, dst, local_sem.at[i])
        copy.start()
        return copy

    def remote(src, dst, device):
        i = counts["remote"]
        counts["remote"] += 1
        copy = pltpu.make_async_remote_copy(
            src_ref=src, dst_ref=dst, send_sem=send_sem.at[i], recv_sem=recv_sem.at[i],
            device_id=device, device_id_type=MESH,
        )
        copy.start()
        sends.append(copy)
        return copy

    order = (far, right, left, x)
    loads = []
    for block in order:
        rows = rows_of(block)
        loads.append((
            local(base.at[rows, own_cols], own_base.at[rows]),
            local(params.at[0, rows, own_cols], own_params.at[rows]),
        ))
    moment_rows = pl.ds(pl.multiple_of(c * 8, 8), 8)
    other_rows = pl.ds(pl.multiple_of((1 - c) * 8, 8), 8)
    moment_load = local(momentum.at[:, own_cols], moment.at[moment_rows])
    oth_base_load = local(base.at[:, oth_cols], oth_base)

    barrier = pltpu.get_barrier_semaphore()
    for device in [sibling, x_right_dev, x_left_dev] + z_devs:
        pl.semaphore_signal(barrier, inc=1, device_id=device, device_id_type=MESH)

    for half in range(2):
        for row in range(2):
            for tile in range(tiles):
                at = (half * 2 + row) * tiles + tile
                column = tile + (c if half == 0 else 1 - c) * tiles
                if half == 0:
                    exps[0, pl.ds(at, 1), :] = jnp.full((1, BLOCK), enc_exp[row, column], jnp.int32)
                exps[1, pl.ds(at, 1), :] = jnp.full((1, BLOCK), ret_exp[row, column], jnp.int32)
    encode_exps = exps[0, 0:2 * tiles, :]
    return_exps = exps[1, 0:4 * tiles, :]
    enc_mul[0:2 * tiles, :] = power_of_two(-encode_exps)
    enc_scale[0:2 * tiles, :] = power_of_two(encode_exps)
    ret_mul[0:4 * tiles, :] = power_of_two(-return_exps)
    ret_scale[0:4 * tiles, :] = power_of_two(return_exps)

    pl.semaphore_wait(barrier, 6)

    swaps = []
    for block in order:
        rows = rows_of(block)
        swaps.append(remote(params.at[0, rows, oth_cols], sib_params.at[rows], sibling))
    moment_swap = remote(momentum.at[:, oth_cols], moment.at[moment_rows], sibling)

    ready = set()

    def need(which):
        if which not in ready:
            ready.add(which)
            for copy in loads[which]:
                copy.wait()
            swaps[which].wait_recv()

    def encoded_pair(which, tile):
        block = order[which]
        rows = rows_of(block)
        lanes = slice(tile * BLOCK, (tile + 1) * BLOCK)
        factor = enc_mul[pl.ds((block // 2) * tiles + tile, 1), :]
        start = own_base[rows, lanes].astype(F32)
        total = None
        for source in (own_params, sib_params):
            code = jnp.clip((source[rows, lanes].astype(F32) - start) * factor, -CODE_LIMIT, CODE_LIMIT)
            code = code.astype(BF16).astype(F32)
            total = code if total is None else total + code
        return total

    state = [dict() for _ in CHUNKS]
    upper, lower = pl.ds(0, HALF), pl.ds(HALF, HALF)

    def far_stage(k):
        lo, hi = CHUNKS[k]
        need(0)
        for tile in range(lo, hi):
            s_far[tile] = encoded_pair(0, tile).astype(BF16)
        part = pl.ds(lo, hi - lo)
        state[k]["up"] = remote(s_far.at[part, upper], f_up.at[part], x_right_dev)
        state[k]["dn"] = remote(s_far.at[part, lower], f_dn.at[part], x_left_dev)

    def near_stage(k):
        lo, hi = CHUNKS[k]
        part = pl.ds(lo, hi - lo)
        need(1)
        for tile in range(lo, hi):
            s_right[tile] = encoded_pair(1, tile).astype(BF16)
        state[k]["raw_r"] = remote(s_right.at[part, lower], x_left.at[part, lower], x_right_dev)
        need(2)
        for tile in range(lo, hi):
            s_left[tile] = encoded_pair(2, tile).astype(BF16)
        state[k]["raw_l"] = remote(s_left.at[part, upper], x_right.at[part, upper], x_left_dev)

    def join_stage(k):
        lo, hi = CHUNKS[k]
        part = pl.ds(lo, hi - lo)
        state[k]["up"].wait_recv()
        for tile in range(lo, hi):
            s_right[tile, 0:HALF] = (s_right[tile, 0:HALF].astype(F32) + f_up[tile].astype(F32)).astype(BF16)
        state[k]["sum_r"] = remote(s_right.at[part, upper], x_left.at[part, upper], x_right_dev)
        state[k]["dn"].wait_recv()
        for tile in range(lo, hi):
            s_left[tile, HALF:XROWS] = (s_left[tile, HALF:XROWS].astype(F32) + f_dn[tile].astype(F32)).astype(BF16)
        state[k]["sum_l"] = remote(s_left.at[part, lower], x_right.at[part, lower], x_left_dev)

    def line_stage(k):
        lo, hi = CHUNKS[k]
        part = pl.ds(lo, hi - lo)
        need(3)
        for name in ("raw_r", "raw_l", "sum_r", "sum_l"):
            state[k][name].wait_recv()
        for tile in range(lo, hi):
            total = encoded_pair(3, tile) + x_left[tile].astype(F32) + x_right[tile].astype(F32)
            t_wide[tile] = total
            t_narrow[tile] = total.astype(BF16)
        state[k]["z"] = []
        for d in (2, 1, 3):
            rows = pl.ds(pl.multiple_of(((z + d) % NZ) * ZROWS, ZROWS), ZROWS)
            state[k]["z"].append(remote(t_narrow.at[part, rows], z_in.at[d - 1, part], z_devs[d - 1]))

    own_rows = pl.ds(pl.multiple_of(z * ZROWS, ZROWS), ZROWS)
    code_rows = pl.ds(pl.multiple_of(x * XROWS + z * ZROWS, ZROWS), ZROWS)

    def step_stage(k):
        lo, hi = CHUNKS[k]
        part = pl.ds(lo, hi - lo)
        if k == 0:
            moment_load.wait()
            moment_swap.wait_recv()
        for copy in state[k]["z"]:
            copy.wait_recv()
        for tile in range(lo, hi):
            lanes = slice(tile * BLOCK, (tile + 1) * BLOCK)
            at = pl.ds((x // 2) * tiles + tile, 1)
            summed = t_wide[tile, own_rows]
            for d in range(3):
                summed = summed + z_in[d, tile].astype(F32)
            outer_grad = summed * (enc_scale[at, :] * (1.0 / 32.0))
            new_moment = MOMENTUM_RATE * moment[:, lanes] + outer_grad
            moment_out[:, lanes] = new_moment
            outer_step = OUTER_RATE * (outer_grad + MOMENTUM_RATE * new_moment)
            code = jnp.clip(outer_step * ret_mul[at, :], -CODE_LIMIT, CODE_LIMIT)
            codes[tile, code_rows] = code.astype(BF16)
        state[k]["zg"] = [
            remote(codes.at[part, code_rows], codes.at[part, code_rows], z_devs[d - 1]) for d in (2, 1, 3)
        ]

    def ring_stage(k):
        lo, hi = CHUNKS[k]
        part = pl.ds(lo, hi - lo)
        for copy in state[k]["zg"]:
            copy.wait_recv()
        up, dn = rows_of(x, 0, HALF), rows_of(x, HALF, HALF)
        st = state[k]
        st["g_ru"] = remote(codes.at[part, up], codes.at[part, up], x_right_dev)
        st["g_ld"] = remote(codes.at[part, dn], codes.at[part, dn], x_left_dev)
        st["g_rd"] = remote(codes.at[part, dn], codes.at[part, dn], x_right_dev)
        st["g_lu"] = remote(codes.at[part, up], codes.at[part, up], x_left_dev)
        rows = rows_of(x)
        st["c"] = [remote(codes.at[part, rows], sib_codes.at[part, rows], sibling)]

    def pass_stage(k):
        lo, hi = CHUNKS[k]
        part = pl.ds(lo, hi - lo)
        st = state[k]
        st["g_ru"].wait_recv()
        rows = rows_of(left, 0, HALF)
        st["p_r"] = remote(codes.at[part, rows], codes.at[part, rows], x_right_dev)
        st["g_ld"].wait_recv()
        rows = rows_of(right, HALF, HALF)
        st["p_l"] = remote(codes.at[part, rows], codes.at[part, rows], x_left_dev)
        st["g_rd"].wait_recv()
        rows = rows_of(left)
        st["c"].append(remote(codes.at[part, rows], sib_codes.at[part, rows], sibling))
        st["g_lu"].wait_recv()
        rows = rows_of(right)
        st["c"].append(remote(codes.at[part, rows], sib_codes.at[part, rows], sibling))

    def last_stage(k):
        lo, hi = CHUNKS[k]
        part = pl.ds(lo, hi - lo)
        st = state[k]
        st["p_r"].wait_recv()
        st["p_l"].wait_recv()
        rows = rows_of(far)
        st["c"].append(remote(codes.at[part, rows], sib_codes.at[part, rows], sibling))

    stores = []
    first_other = []

    def apply(k, block, own):
        lo, hi = CHUNKS[k]
        rows = rows_of(block)
        if not own and not first_other:
            first_other.append(True)
            oth_base_load.wait()
        source, start, out = (codes, own_base, own_out) if own else (sib_codes, oth_base, oth_out)
        for tile in range(lo, hi):
            lanes = slice(tile * BLOCK, (tile + 1) * BLOCK)
            at = pl.ds(((0 if own else 2) + block // 2) * tiles + tile, 1)
            update = source[tile, rows].astype(F32) * ret_scale[at, :]
            out[rows, lanes] = (start[rows, lanes].astype(F32) + update).astype(BF16)
        columns = pl.ds(
            pl.multiple_of((c if own else 1 - c) * width + lo * BLOCK, BLOCK), (hi - lo) * BLOCK
        )
        stores.append(local(
            out.at[rows, pl.ds(lo * BLOCK, (hi - lo) * BLOCK)], new_params.at[rows, columns]
        ))

    def apply_other(k, i):
        state[k]["c"][i].wait_recv()
        apply(k, (x, left, right, far)[i], False)

    far_stage(0)
    far_stage(1)
    far_stage(2)
    near_stage(0)
    near_stage(1)
    join_stage(0)
    near_stage(2)
    join_stage(1)
    line_stage(0)
    join_stage(2)
    line_stage(1)
    step_stage(0)
    line_stage(2)
    step_stage(1)
    ring_stage(0)
    step_stage(2)
    ring_stage(1)
    back = remote(moment_out.at[other_rows], moment_in, sibling)
    stores.append(local(moment_out.at[moment_rows], new_momentum.at[:, own_cols]))
    pass_stage(0)
    ring_stage(2)
    apply(0, x, True)
    apply(1, x, True)
    apply(0, left, True)
    apply(0, right, True)
    pass_stage(1)
    last_stage(0)
    back.wait_recv()
    stores.append(local(moment_in, new_momentum.at[:, oth_cols]))
    apply(2, x, True)
    apply_other(0, 0)
    apply_other(1, 0)
    apply_other(2, 0)
    apply_other(0, 1)
    apply_other(0, 2)
    pass_stage(2)
    last_stage(1)
    apply(0, far, True)
    apply_other(0, 3)
    apply(1, left, True)
    apply(1, right, True)
    apply_other(1, 1)
    apply_other(1, 2)
    apply(2, left, True)
    apply(2, right, True)
    apply(1, far, True)
    apply_other(1, 3)
    last_stage(2)
    apply_other(2, 1)
    apply_other(2, 2)
    apply(2, far, True)
    apply_other(2, 3)

    for copy in sends:
        copy.wait_send()
    for copy in stores:
        copy.wait()


def on_device(local_params, base_params, momentum, encode_exponents, return_exponents):
    _, rows, columns = local_params.shape
    width = columns // 2
    tiles = width // BLOCK
    table = pltpu.VMEM((-(-4 * tiles // 8) * 8, BLOCK), F32)
    half = pltpu.VMEM((rows, width), BF16)
    block = pltpu.VMEM((tiles, XROWS, BLOCK), BF16)
    half_block = pltpu.VMEM((tiles, HALF, BLOCK), BF16)
    any_space = pl.BlockSpec(memory_space=pltpu.HBM)
    scalars = pl.BlockSpec(memory_space=pltpu.SMEM)
    return pl.pallas_call(
        kernel,
        name="outer_step",
        out_shape=(
            jax.ShapeDtypeStruct((rows, columns), BF16),
            jax.ShapeDtypeStruct(momentum.shape, F32),
        ),
        in_specs=[any_space, any_space, any_space, scalars, scalars],
        out_specs=(any_space, any_space),
        scratch_shapes=[
            half, half, half, half,
            pltpu.VMEM((2, -(-4 * tiles // 8) * 8, BLOCK), jnp.int32),
            table, table, table, table,
            block, block, block, half_block, half_block, block, block,
            pltpu.VMEM((tiles, XROWS, BLOCK), F32),
            block,
            pltpu.VMEM((3, tiles, ZROWS, BLOCK), BF16),
            pltpu.VMEM((ZROWS, width), F32),
            pltpu.VMEM((ZROWS, width), F32),
            pltpu.VMEM((8, width), F32),
            pltpu.VMEM((tiles, rows, BLOCK), BF16),
            pltpu.VMEM((tiles, rows, BLOCK), BF16),
            half, half,
            pltpu.SemaphoreType.DMA((48,)),
            pltpu.SemaphoreType.DMA((96,)),
            pltpu.SemaphoreType.DMA((96,)),
        ],
        compiler_params=pltpu.CompilerParams(
            collective_id=0, has_side_effects=True, vmem_limit_bytes=32 * 2**20
        ),
        cost_estimate=pl.CostEstimate(flops=20_000_000, bytes_accessed=4_500_000, transcendentals=0),
    )(local_params, base_params, momentum, encode_exponents, return_exponents)


def solution(mesh):
    return jax.shard_map(
        on_device,
        mesh=mesh,
        in_specs=(
            P("rep", None, "fsdp"),
            P(None, "fsdp"),
            P("rep", "fsdp"),
            P(None, "fsdp"),
            P(None, "fsdp"),
        ),
        out_specs=(P(None, "fsdp"), P("rep", "fsdp")),
        check_vma=False,
    )
```

time: 254 us -> 48.1 us (0.19)
  waiting for transfers between devices: 205 us -> 0 us
  Pallas kernels: 0 us -> 40.5 us
  local copies, waits for them, and re-layouts: 26.8 us -> 6.7 us
  between operations: 14.1 us -> 0.65 us
  other arithmetic: 7.84 us -> 0 us
    reduce_scatter x1 -> x0, waiting for transfers between devices: 140 us -> none  [sync_piece(): lax.psum_scatter(encoded.astype(jnp.float32), 'rep', scatter_dimension=0,...]
    all_gather x1 -> x0, waiting for transfers between devices: 64.8 us -> none  [sync_piece(): all_codes = lax.all_gather(delta_code, 'rep', axis=0, tiled=True)]
    pallas_call x0 -> x1, Pallas kernels: none -> 40.5 us  [on_device(): pl.pallas_call(kernel, name='outer_step', out_shape=(jax.ShapeDtypeStruct...]
    unnamed x18 -> x12, local copies, waits for them, and re-layouts: 18.2 us -> 6.7 us
    convert_element_type x3 -> x0, other arithmetic: 7.05 us -> none  [the longest x1 3.31 us: sync_piece(): (base_wide + all_codes.astype(jnp.float32) * scale_out).astype(jnp.bfloat16)]
    dynamic_slice x1 -> x0, local copies, waits for them, and re-layouts: 4.25 us -> none  [sync_piece(): own_out = lax.dynamic_slice_in_dim(scale_out, first_row, owned_rows, 0)]
  transfers between devices with their start and end apart: 2 -> 0, of which waited for: 2 -> 0; matrix products, arithmetic and copies ran while one was open for 5% -> 0% of each run, Pallas kernels for 0% -> 0%
where the time goes in v1:
time: 48.1 us; the launch traced here: 47.9 us
  Pallas kernels  40.5 us (84%)
  local copies, waits for them, and re-layouts  6.7 us (14%)
  between operations  0.65 us (1%)
    pallas_call x1, Pallas kernels, on_device(): pl.pallas_call(kernel, name='outer_step', out_shape=(jax.ShapeDtypeStruct...  40.5 us
    unnamed x12, local copies, waits for them, and re-layouts  6.7 us

profile of v1, /device:TPU:1, one launch (start us, length us, event | category | flops | bytes accessed | tf_op | source)
XLA Modules:
  0.0 47.9 jit_solution(6438377562527237544)
XLA Ops:
  0.6 0.0 copy-start
  0.6 1.4 %copy-done = bf16[1,256,2816]{2,1,0:T(8,128)(2,1)S(1)} copy-done((bf16[1,256,2816]{2,1,0:T(8,128)(2,1)S(1)}, bf16[1,256,2816]{2,1,0:T(8,128)(2,1)}, u32[]{:S(2)}) %copy-start) | copy-done | bytes 1441816
  2.0 0.0 copy-start.1
  2.0 1.4 %copy-done.1 = bf16[256,2816]{1,0:T(8,128)(2,1)S(1)} copy-done((bf16[256,2816]{1,0:T(8,128)(2,1)S(1)}, bf16[256,2816]{1,0:T(8,128)(2,1)}, u32[]{:S(2)}) %copy-start.1) | copy-done | bytes 1441816
  3.4 0.0 copy-start.2
  3.4 0.9 %copy-done.2 = f32[8,2816]{1,0:T(8,128)S(1)} copy-done((f32[8,2816]{1,0:T(8,128)S(1)}, f32[8,2816]{1,0:T(8,128)}, u32[]{:S(2)}) %copy-start.2) | copy-done | bytes 90136
  4.2 0.0 copy-start.3
  4.2 0.7 %copy-done.3 = s32[2,22]{1,0:T(2,128)S(1)} copy-done((s32[2,22]{1,0:T(2,128)S(1)}, s32[2,22]{1,0:T(2,128)}, u32[]{:S(2)}) %copy-start.3) | copy-done | bytes 200
  4.9 0.0 copy-start.4
  4.9 0.7 %copy-done.4 = s32[2,22]{1,0:T(2,128)S(1)} copy-done((s32[2,22]{1,0:T(2,128)S(1)}, s32[2,22]{1,0:T(2,128)}, u32[]{:S(2)}) %copy-start.4) | copy-done | bytes 200
  5.6 40.5 %outer_step.1 = (bf16[256,2816]{1,0:T(8,128)(2,1)S(1)}, f32[8,2816]{1,0:T(8,128)S(1)}) custom-call(bf16[1,256,2816]{2,1,0:T(8,128)(2,1)S(1)} %copy-done, bf16[256,2816]{1,0:T(8,128)(2,1)S(1)} %copy-done.1, f32[8,2816]{1,0:T(8,128)S(1)} %copy-done.2, s32[2,22]{1,0:T(2,128)S(1)} %copy-done.3, s32[2,22]{1,0:T(2,128)S(1)} %copy-done.4), custom_call_target="tpu_custom_call" | custom-call | flops 20000000 | bytes 4500000 | tf_op jit(solution)/shard_map/outer_step/pallas_call | solution.py:354
  46.1 1.1 %copy.9 = bf16[256,2816]{1,0:T(8,128)(2,1)} copy(bf16[256,2816]{1,0:T(8,128)(2,1)S(1)} %get-tuple-element.4) | data formatting | bytes 2883584
  47.2 0.6 %copy.10 = f32[8,2816]{1,0:T(8,128)} copy(f32[8,2816]{1,0:T(8,128)S(1)} %get-tuple-element.5) | data formatting | bytes 180224
Async XLA Ops:
  0.6 1.4 %copy-start = (bf16[1,256,2816]{2,1,0:T(8,128)(2,1)S(1)}, bf16[1,256,2816]{2,1,0:T(8,128)(2,1)}, u32[]{:S(2)}) copy-start(bf16[1,256,2816]{2,1,0:T(8,128)(2,1)} %params.1) | copy-start | bytes 4325380
  2.0 1.4 %copy-start.1 = (bf16[256,2816]{1,0:T(8,128)(2,1)S(1)}, bf16[256,2816]{1,0:T(8,128)(2,1)}, u32[]{:S(2)}) copy-start(bf16[256,2816]{1,0:T(8,128)(2,1)} %base.1) | copy-start | bytes 4325380
  3.4 0.9 %copy-start.2 = (f32[8,2816]{1,0:T(8,128)S(1)}, f32[8,2816]{1,0:T(8,128)}, u32[]{:S(2)}) copy-start(f32[8,2816]{1,0:T(8,128)} %momentum.1) | copy-start | bytes 270340
  4.2 0.7 %copy-start.3 = (s32[2,22]{1,0:T(2,128)S(1)}, s32[2,22]{1,0:T(2,128)}, u32[]{:S(2)}) copy-start(s32[2,22]{1,0:T(2,128)} %enc_exp.1) | copy-start | bytes 532
  4.9 0.7 %copy-start.4 = (s32[2,22]{1,0:T(2,128)S(1)}, s32[2,22]{1,0:T(2,128)}, u32[]{:S(2)}) copy-start(s32[2,22]{1,0:T(2,128)} %ret_exp.1) | copy-start | bytes 532

commit v2 on v0

v2 whole, which is shorter than its diff:
```python
import jax
import jax.numpy as jnp
from jax import lax
from jax.experimental import pallas as pl
from jax.experimental.pallas import tpu as pltpu
from jax.sharding import PartitionSpec as P

BLOCK = 128
CODE_LIMIT = 448.0
MOMENTUM_RATE = 0.9
OUTER_RATE = 0.7
MESH = pl.DeviceIdType.MESH
NX, NZ = 4, 4
XROWS, ZROWS = 64, 16
HALF = XROWS // 2
CHUNKS = ((0, 4), (4, 8), (8, 11))
BF16, F32 = jnp.bfloat16, jnp.float32
LOADS = ("block0", "block1", "block2", "block3", "exponents", "other_base", "params_out", "moment_out")
SENDS = ("swap", "moment", "far", "right", "left", "line", "codes", "ring", "pass", "core", "moment_back")
ARRIVALS = ("swap0", "swap1", "swap2", "swap3", "moment", "moment_back") + tuple(
    f"{name}{k}"
    for k in range(len(CHUNKS))
    for name in ("up", "dn", "x", "line", "codes", "ring_r", "ring_l", "ring_n", "pass", "core_own", "core_near", "core_far")
)
SCHEDULE = (
    ("far", 0),
    ("far", 1),
    ("far", 2),
    ("near", 0),
    ("near", 1),
    ("join", 0),
    ("near", 2),
    ("join", 1),
    ("line", 0),
    ("join", 2),
    ("line", 1),
    ("step", 0),
    ("line", 2),
    ("step", 1),
    ("ring", 0),
    ("step", 2),
    ("ring", 1),
    ("moment_out",),
    ("pass", 0),
    ("ring", 2),
    ("own", 0, 0),
    ("own", 1, 0),
    ("own", 0, 1),
    ("own", 0, 2),
    ("pass", 1),
    ("last", 0),
    ("moment_in",),
    ("own", 2, 0),
    ("other", 0, 0),
    ("other", 1, 0),
    ("other", 2, 0),
    ("other", 0, 1),
    ("other", 0, 2),
    ("pass", 2),
    ("last", 1),
    ("own", 0, 3),
    ("other", 0, 3),
    ("own", 1, 1),
    ("own", 1, 2),
    ("other", 1, 1),
    ("other", 1, 2),
    ("own", 2, 1),
    ("own", 2, 2),
    ("own", 1, 3),
    ("other", 1, 3),
    ("last", 2),
    ("other", 2, 1),
    ("other", 2, 2),
    ("own", 2, 3),
    ("other", 2, 3),
)


def power_of_two(exponent):
    size = jnp.abs(exponent)
    result = jnp.ones(exponent.shape, F32)
    for bit in range(7):
        up, down = 2.0 ** (1 << bit), 2.0 ** -(1 << bit)
        factor = jnp.where(exponent < 0, down, up)
        result = result * jnp.where((size & (1 << bit)) != 0, factor, 1.0)
    return result


def kernel(
    params, base, momentum, enc_exp, ret_exp, new_params, new_momentum,
    exp_words, mine, sib_params, oth_base, exps, enc_mul, enc_scale, ret_mul, ret_scale,
    s_far, s_right, s_left, f_up, f_dn, x_in, t_wide, t_narrow, z_in,
    moment, moment_out, moment_in, codes, sib_codes, own_out, oth_out,
    load_sem, send_sem, recv_sem,
):
    rep = lax.axis_index("rep")
    x, z, c = rep // (NZ * 2), (rep // 2) % NZ, rep % 2
    width = sib_params.shape[1]
    tiles = width // BLOCK

    def place(px, pz, pc):
        return {"rep": (px * NZ + pz) * 2 + pc}

    sibling = place(x, z, 1 - c)
    right, left, far = (x + 1) % NX, (x + 3) % NX, (x + 2) % NX
    x_right_dev, x_left_dev = place(right, z, c), place(left, z, c)
    z_devs = [place(x, (z + d) % NZ, c) for d in (1, 2, 3)]

    def rows_of(block, first=0, count=XROWS):
        return pl.ds(pl.multiple_of(block * XROWS + first, 16), count)

    own_cols = pl.ds(pl.multiple_of(c * width, BLOCK), width)
    oth_cols = pl.ds(pl.multiple_of((1 - c) * width, BLOCK), width)

    def local(src, dst, name):
        pltpu.make_async_copy(src, dst, load_sem.at[LOADS.index(name)]).start()

    def remote(src, dst, device, send, arrival):
        pltpu.make_async_remote_copy(
            src_ref=src, dst_ref=dst, send_sem=send_sem.at[SENDS.index(send)],
            recv_sem=recv_sem.at[ARRIVALS.index(arrival)], device_id=device, device_id_type=MESH,
        ).start()

    def take(sem, ref):
        pltpu.make_async_copy(ref, ref, sem).wait()

    def loaded(name, ref):
        take(load_sem.at[LOADS.index(name)], ref)

    def arrived(name, ref):
        take(recv_sem.at[ARRIVALS.index(name)], ref)

    def sent(name, ref):
        take(send_sem.at[SENDS.index(name)], ref)

    local(enc_exp, exp_words.at[0], "exponents")
    local(ret_exp, exp_words.at[1], "exponents")
    order = (far, right, left, x)
    for which, block in enumerate(order):
        rows = rows_of(block)
        local(base.at[rows, own_cols], mine.at[0, rows], f"block{which}")
        local(params.at[0, rows, own_cols], mine.at[1, rows], f"block{which}")

    barrier = pltpu.get_barrier_semaphore()
    for device in [x_right_dev, x_left_dev] + z_devs + [sibling]:
        pl.semaphore_signal(barrier, inc=1, device_id=device, device_id_type=MESH)

    loaded("exponents", exp_words)
    for half in range(2):
        for row in range(2):
            for tile in range(tiles):
                at = (half * 2 + row) * tiles + tile
                column = tile + (c if half == 0 else 1 - c) * tiles
                if half == 0:
                    exps[0, pl.ds(at, 1), :] = jnp.full((1, BLOCK), exp_words[0, row, column], jnp.int32)
                exps[1, pl.ds(at, 1), :] = jnp.full((1, BLOCK), exp_words[1, row, column], jnp.int32)
    encode_exps = exps[0, 0:2 * tiles, :]
    return_exps = exps[1, 0:4 * tiles, :]
    enc_mul[0:2 * tiles, :] = power_of_two(-encode_exps)
    enc_scale[0:2 * tiles, :] = power_of_two(encode_exps)
    ret_mul[0:4 * tiles, :] = power_of_two(-return_exps)
    ret_scale[0:4 * tiles, :] = power_of_two(return_exps)

    pl.semaphore_wait(barrier, 6)

    for which, block in enumerate(order):
        rows = rows_of(block)
        remote(params.at[0, rows, oth_cols], sib_params.at[rows], sibling, "swap", f"swap{which}")
    moment_rows = pl.ds(pl.multiple_of(c * 8, 8), 8)
    other_rows = pl.ds(pl.multiple_of((1 - c) * 8, 8), 8)
    remote(momentum.at[:, oth_cols], moment.at[moment_rows], sibling, "moment", "moment")
    moment_load = pltpu.make_async_copy(
        momentum.at[:, own_cols], moment.at[moment_rows], recv_sem.at[ARRIVALS.index("moment")]
    )
    moment_load.start()
    local(base.at[:, oth_cols], oth_base, "other_base")

    ready = set()

    def need(which):
        if which not in ready:
            ready.add(which)
            rows = rows_of(order[which])
            loaded(f"block{which}", mine.at[:, rows])
            arrived(f"swap{which}", sib_params.at[rows])

    def encoded_pair(which, tile):
        block = order[which]
        rows = rows_of(block)
        lanes = slice(tile * BLOCK, (tile + 1) * BLOCK)
        factor = enc_mul[pl.ds((block // 2) * tiles + tile, 1), :]
        start = mine[0, rows, lanes].astype(F32)
        total = None
        for source in (mine[1, rows, lanes], sib_params[rows, lanes]):
            code = jnp.clip((source.astype(F32) - start) * factor, -CODE_LIMIT, CODE_LIMIT)
            code = code.astype(BF16).astype(F32)
            total = code if total is None else total + code
        return total

    upper, lower = pl.ds(0, HALF), pl.ds(HALF, HALF)

    def part_of(k):
        lo, hi = CHUNKS[k]
        return range(lo, hi), pl.ds(lo, hi - lo)

    def far_stage(k):
        need(0)
        span, part = part_of(k)
        for tile in span:
            s_far[tile] = encoded_pair(0, tile).astype(BF16)
        remote(s_far.at[part, upper], f_up.at[part], x_right_dev, "far", f"up{k}")
        remote(s_far.at[part, lower], f_dn.at[part], x_left_dev, "far", f"dn{k}")

    def near_stage(k):
        span, part = part_of(k)
        need(1)
        for tile in span:
            s_right[tile] = encoded_pair(1, tile).astype(BF16)
        remote(s_right.at[part, lower], x_in.at[0, part, lower], x_right_dev, "right", f"x{k}")
        need(2)
        for tile in span:
            s_left[tile] = encoded_pair(2, tile).astype(BF16)
        remote(s_left.at[part, upper], x_in.at[1, part, upper], x_left_dev, "left", f"x{k}")

    def join_stage(k):
        span, part = part_of(k)
        arrived(f"up{k}", f_up.at[part])
        for tile in span:
            s_right[tile, 0:HALF] = (s_right[tile, 0:HALF].astype(F32) + f_up[tile].astype(F32)).astype(BF16)
        remote(s_right.at[part, upper], x_in.at[0, part, upper], x_right_dev, "right", f"x{k}")
        arrived(f"dn{k}", f_dn.at[part])
        for tile in span:
            s_left[tile, HALF:XROWS] = (s_left[tile, HALF:XROWS].astype(F32) + f_dn[tile].astype(F32)).astype(BF16)
        remote(s_left.at[part, lower], x_in.at[1, part, lower], x_left_dev, "left", f"x{k}")

    def line_stage(k):
        span, part = part_of(k)
        need(3)
        arrived(f"x{k}", x_in.at[:, part])
        for tile in span:
            total = encoded_pair(3, tile) + x_in[0, tile].astype(F32) + x_in[1, tile].astype(F32)
            t_wide[tile] = total
            t_narrow[tile] = total.astype(BF16)
        for d in (2, 1, 3):
            rows = pl.ds(pl.multiple_of(((z + d) % NZ) * ZROWS, ZROWS), ZROWS)
            remote(t_narrow.at[part, rows], z_in.at[d - 1, part], z_devs[d - 1], "line", f"line{k}")

    own_rows = pl.ds(pl.multiple_of(z * ZROWS, ZROWS), ZROWS)
    code_rows = pl.ds(pl.multiple_of(x * XROWS + z * ZROWS, ZROWS), ZROWS)

    def step_stage(k):
        span, part = part_of(k)
        if k == 0:
            arrived("moment", moment)
        arrived(f"line{k}", z_in.at[:, part])
        for tile in span:
            lanes = slice(tile * BLOCK, (tile + 1) * BLOCK)
            at = pl.ds((x // 2) * tiles + tile, 1)
            summed = t_wide[tile, own_rows]
            for d in range(3):
                summed = summed + z_in[d, tile].astype(F32)
            outer_grad = summed * (enc_scale[at, :] * (1.0 / 32.0))
            new_moment = MOMENTUM_RATE * moment[:, lanes] + outer_grad
            moment_out[:, lanes] = new_moment
            outer_step = OUTER_RATE * (outer_grad + MOMENTUM_RATE * new_moment)
            code = jnp.clip(outer_step * ret_mul[at, :], -CODE_LIMIT, CODE_LIMIT)
            codes[tile, code_rows] = code.astype(BF16)
        mine_now = codes.at[part, code_rows]
        for d in (2, 1, 3):
            remote(mine_now, mine_now, z_devs[d - 1], "codes", f"codes{k}")

    def gathered(k, block, first=0, count=XROWS):
        return codes.at[part_of(k)[1], rows_of(block, first, count)]

    def to_sibling(k, block, arrival):
        part, rows = part_of(k)[1], rows_of(block)
        remote(codes.at[part, rows], sib_codes.at[part, rows], sibling, "core", arrival)

    def ring_stage(k):
        arrived(f"codes{k}", z_in.at[:, part_of(k)[1]])
        up, dn = gathered(k, x, 0, HALF), gathered(k, x, HALF, HALF)
        remote(up, up, x_right_dev, "ring", f"ring_r{k}")
        remote(dn, dn, x_left_dev, "ring", f"ring_l{k}")
        remote(dn, dn, x_right_dev, "ring", f"ring_n{k}")
        remote(up, up, x_left_dev, "ring", f"ring_n{k}")
        to_sibling(k, x, f"core_own{k}")

    def pass_stage(k):
        up, dn = gathered(k, left, 0, HALF), gathered(k, right, HALF, HALF)
        arrived(f"ring_r{k}", up)
        remote(up, up, x_right_dev, "pass", f"pass{k}")
        arrived(f"ring_l{k}", dn)
        remote(dn, dn, x_left_dev, "pass", f"pass{k}")
        arrived(f"ring_n{k}", gathered(k, x))
        to_sibling(k, left, f"core_near{k}")
        to_sibling(k, right, f"core_near{k}")

    def last_stage(k):
        arrived(f"pass{k}", gathered(k, far))
        to_sibling(k, far, f"core_far{k}")

    def apply(k, block, own):
        span, part = part_of(k)
        rows = rows_of(block)
        if not own and "other_base" not in ready:
            ready.add("other_base")
            loaded("other_base", oth_base)
        out = own_out if own else oth_out
        for tile in span:
            lanes = slice(tile * BLOCK, (tile + 1) * BLOCK)
            at = pl.ds(((0 if own else 2) + block // 2) * tiles + tile, 1)
            code = (codes if own else sib_codes)[tile, rows].astype(F32)
            start = mine[0, rows, lanes] if own else oth_base[rows, lanes]
            out[rows, lanes] = (start.astype(F32) + code * ret_scale[at, :]).astype(BF16)
        first, count = span.start * BLOCK, len(span) * BLOCK
        columns = pl.ds(pl.multiple_of((c if own else 1 - c) * width + first, BLOCK), count)
        local(out.at[rows, pl.ds(first, count)], new_params.at[rows, columns], "params_out")

    def own_stage(k, i):
        apply(k, (x, left, right, far)[i], True)

    def other_stage(k, i):
        if i == 0:
            arrived(f"core_own{k}", gathered(k, x))
        elif i == 1:
            arrived(f"core_near{k}", codes.at[part_of(k)[1], pl.ds(0, 2 * XROWS)])
        elif i == 3:
            arrived(f"core_far{k}", gathered(k, x))
        apply(k, (x, left, right, far)[i], False)

    def send_moment():
        remote(moment_out.at[other_rows], moment_in, sibling, "moment_back", "moment_back")
        local(moment_out.at[moment_rows], new_momentum.at[:, own_cols], "moment_out")

    def take_moment():
        arrived("moment_back", moment_in)
        local(moment_in, new_momentum.at[:, oth_cols], "moment_out")

    stages = {
        "far": far_stage, "near": near_stage, "join": join_stage, "line": line_stage, "step": step_stage,
        "ring": ring_stage, "pass": pass_stage, "last": last_stage, "own": own_stage, "other": other_stage,
        "moment_out": send_moment, "moment_in": take_moment,
    }
    for name, *where in SCHEDULE:
        stages[name](*where)

    sent("swap", sib_params)
    sent("moment", moment_in)
    sent("far", s_far)
    sent("right", s_right)
    sent("left", s_left)
    sent("line", z_in)
    sent("codes", z_in)
    sent("ring", codes.at[:, pl.ds(0, 2 * XROWS)])
    sent("pass", codes.at[:, pl.ds(0, XROWS)])
    sent("core", codes)
    sent("moment_back", moment_in)
    loaded("params_out", new_params)
    loaded("moment_out", new_momentum)


def on_device(local_params, base_params, momentum, encode_exponents, return_exponents):
    _, rows, columns = local_params.shape
    width = columns // 2
    tiles = width // BLOCK
    table = pltpu.VMEM((-(-4 * tiles // 8) * 8, BLOCK), F32)
    half = pltpu.VMEM((rows, width), BF16)
    block = pltpu.VMEM((tiles, XROWS, BLOCK), BF16)
    half_block = pltpu.VMEM((tiles, HALF, BLOCK), BF16)
    any_space = pl.BlockSpec(memory_space=pltpu.HBM)
    return pl.pallas_call(
        kernel,
        name="outer_step",
        out_shape=(
            jax.ShapeDtypeStruct((rows, columns), BF16),
            jax.ShapeDtypeStruct(momentum.shape, F32),
        ),
        in_specs=[any_space] * 5,
        out_specs=(any_space, any_space),
        scratch_shapes=[
            pltpu.SMEM((2,) + encode_exponents.shape, jnp.int32),
            pltpu.VMEM((2, rows, width), BF16),
            half, half,
            pltpu.VMEM((2, -(-4 * tiles // 8) * 8, BLOCK), jnp.int32),
            table, table, table, table,
            block, block, block, half_block, half_block,
            pltpu.VMEM((2, tiles, XROWS, BLOCK), BF16),
            pltpu.VMEM((tiles, XROWS, BLOCK), F32),
            block,
            pltpu.VMEM((3, tiles, ZROWS, BLOCK), BF16),
            pltpu.VMEM((ZROWS, width), F32),
            pltpu.VMEM((ZROWS, width), F32),
            pltpu.VMEM((8, width), F32),
            pltpu.VMEM((tiles, rows, BLOCK), BF16),
            pltpu.VMEM((tiles, rows, BLOCK), BF16),
            half, half,
            pltpu.SemaphoreType.DMA((len(LOADS),)),
            pltpu.SemaphoreType.DMA((len(SENDS),)),
            pltpu.SemaphoreType.DMA((len(ARRIVALS),)),
        ],
        compiler_params=pltpu.CompilerParams(
            collective_id=0, has_side_effects=True, vmem_limit_bytes=32 * 2**20
        ),
        cost_estimate=pl.CostEstimate(flops=20_000_000, bytes_accessed=4_500_000, transcendentals=0),
    )(*[
        pltpu.with_memory_space_constraint(array, pltpu.HBM)
        for array in (local_params, base_params, momentum, encode_exponents, return_exponents)
    ])


def solution(mesh):
    return jax.shard_map(
        on_device,
        mesh=mesh,
        in_specs=(
            P("rep", None, "fsdp"),
            P(None, "fsdp"),
            P("rep", "fsdp"),
            P(None, "fsdp"),
            P(None, "fsdp"),
        ),
        out_specs=(P(None, "fsdp"), P("rep", "fsdp")),
        check_vma=False,
    )
```

time: 254 us -> 40.6 us (0.16)
  waiting for transfers between devices: 205 us -> 0 us
  Pallas kernels: 0 us -> 38.1 us
  local copies, waits for them, and re-layouts: 26.8 us -> 1.74 us
  between operations: 14.1 us -> 0.64 us
  other arithmetic: 7.84 us -> 0 us
    reduce_scatter x1 -> x0, waiting for transfers between devices: 140 us -> none  [sync_piece(): lax.psum_scatter(encoded.astype(jnp.float32), 'rep', scatter_dimension=0,...]
    all_gather x1 -> x0, waiting for transfers between devices: 64.8 us -> none  [sync_piece(): all_codes = lax.all_gather(delta_code, 'rep', axis=0, tiled=True)]
    pallas_call x0 -> x1, Pallas kernels: none -> 38.1 us  [on_device(): pl.pallas_call(kernel, name='outer_step', out_shape=(jax.ShapeDtypeStruct...]
    unnamed x18 -> x2, local copies, waits for them, and re-layouts: 18.2 us -> 1.74 us
    convert_element_type x3 -> x0, other arithmetic: 7.05 us -> none  [the longest x1 3.31 us: sync_piece(): (base_wide + all_codes.astype(jnp.float32) * scale_out).astype(jnp.bfloat16)]
    dynamic_slice x1 -> x0, local copies, waits for them, and re-layouts: 4.25 us -> none  [sync_piece(): own_out = lax.dynamic_slice_in_dim(scale_out, first_row, owned_rows, 0)]
  transfers between devices with their start and end apart: 2 -> 0, of which waited for: 2 -> 0; matrix products, arithmetic and copies ran while one was open for 5% -> 0% of each run, Pallas kernels for 0% -> 0%
where the time goes in v2:
time: 40.6 us; the launch traced here: 40.5 us
  Pallas kernels  38.1 us (94%)
  local copies, waits for them, and re-layouts  1.74 us (4%)
  between operations  0.64 us (2%)
    pallas_call x1, Pallas kernels, on_device(): pl.pallas_call(kernel, name='outer_step', out_shape=(jax.ShapeDtypeStruct...  38.1 us
    unnamed x2, local copies, waits for them, and re-layouts  1.74 us

profile of v2, /device:TPU:1, one launch (start us, length us, event | category | flops | bytes accessed | tf_op | source)
XLA Modules:
  0.0 40.5 jit_solution(8919774920532722387)
XLA Ops:
  0.6 38.1 %outer_step.1 = (bf16[256,2816]{1,0:T(8,128)(2,1)S(1)}, f32[8,2816]{1,0:T(8,128)S(1)}) custom-call(bf16[1,256,2816]{2,1,0:T(8,128)(2,1)} %params.1, bf16[256,2816]{1,0:T(8,128)(2,1)} %base.1, f32[8,2816]{1,0:T(8,128)} %momentum.1, s32[2,22]{1,0:T(2,128)} %enc_exp.1, s32[2,22]{1,0:T(2,128)} %ret_exp.1), custom_call_target="tpu_custom_call" | custom-call | flops 20000000 | bytes 4500000 | tf_op jit(solution)/shard_map/outer_step/pallas_call | solution.py:371
  38.8 1.1 %copy.9 = bf16[256,2816]{1,0:T(8,128)(2,1)} copy(bf16[256,2816]{1,0:T(8,128)(2,1)S(1)} %get-tuple-element.4) | data formatting | bytes 2883584
  39.9 0.6 %copy.10 = f32[8,2816]{1,0:T(8,128)} copy(f32[8,2816]{1,0:T(8,128)S(1)} %get-tuple-element.5) | data formatting | bytes 180224

commit v3 on v0

v3 whole, which is shorter than its diff:
```python
import jax
import jax.numpy as jnp
from jax import lax
from jax.experimental import pallas as pl
from jax.experimental.pallas import tpu as pltpu
from jax.sharding import PartitionSpec as P

BLOCK = 128
CODE_LIMIT = 448.0
MOMENTUM_RATE = 0.9
OUTER_RATE = 0.7
MESH = pl.DeviceIdType.MESH
BF16, F32 = jnp.bfloat16, jnp.float32
NX, NZ = 4, 4
ZROWS = 16
XROWS = NZ * ZROWS

ONE, TWO, ZFIRST = range(3)
CHUNKS = ((0, 3, ONE), (3, 6, ONE), (6, 9, TWO), (9, 11, ZFIRST))
BLOCKS, EXPONENTS, OTHER_BASE = 0, 4, 5
LOADS = 6
SWAP, SHARDS, SUMS, CODES, GATHER, CORE, MOMENT = range(7)
SENDS = 7
IN_SWAP, IN_MOMENT, IN_MOMENT_BACK, IN_CHUNKS = 0, 4, 5, 6
UP, DOWN, FIRST, SECOND, CODES_IN, NEAR_IN, FAR_IN, CORE_NEAR, CORE_FAR = range(9)
ARRIVALS = IN_CHUNKS + 9 * len(CHUNKS)
ENCODE, SEND_FAR, SEND_NEAR, JOIN, SUM, STEP, RING, LAND_NEAR, LAND, OWN, OWN_NEAR, OWN_FAR, OTHER_NEAR, OTHER_FAR = range(14)
SCHEDULE = (
    (SEND_FAR, 2), (ENCODE, 0), (ENCODE, 1), (SEND_NEAR, 2), (ENCODE, 3),
    (JOIN, 2), (SUM, 0), (SUM, 1), (SUM, 3), (SUM, 2),
    (STEP, 0), (STEP, 3), (STEP, 1), (STEP, 2), (RING, 0),
    (OWN, 0), (RING, 3), (RING, 1), (OWN, 1), (RING, 2),
    (OWN, 2), (LAND, 0), (OWN_FAR, 0), (LAND_NEAR, 0), (OWN_NEAR, 0),
    (OTHER_FAR, 0), (OTHER_NEAR, 0), (LAND, 1), (OWN_FAR, 1), (LAND_NEAR, 1),
    (LAND, 3), (OWN_NEAR, 1), (OWN_FAR, 3), (OTHER_FAR, 1), (OTHER_NEAR, 1),
    (OTHER_FAR, 3), (LAND, 2), (OWN_FAR, 2), (LAND_NEAR, 2), (OWN_NEAR, 2),
    (OTHER_FAR, 2), (OTHER_NEAR, 2),
)


def power_of_two(exponent):
    size = jnp.abs(exponent)
    result = jnp.ones(exponent.shape, F32)
    for bit in range(7):
        up, down = 2.0 ** (1 << bit), 2.0 ** -(1 << bit)
        factor = jnp.where(exponent < 0, down, up)
        result = result * jnp.where((size & (1 << bit)) != 0, factor, 1.0)
    return result


def kernel(
    params, base, momentum, enc_exp, ret_exp, new_params, new_momentum,
    exp_words, mine, sib_params, oth_base, exps, enc_mul, enc_scale, ret_mul, ret_scale,
    shards, up_in, down_in, x_in, z_in, t_wide, t_narrow, moment, moment_out, codes, sib_codes,
    load_sem, send_sem, recv_sem,
):
    rep = lax.axis_index("rep")
    x, z, c = rep // (NZ * 2), (rep // 2) % NZ, rep % 2
    width = sib_params.shape[1]
    tiles = width // BLOCK

    def place(px, pz, pc):
        return {"rep": (px * NZ + pz) * 2 + pc}

    sibling = place(x, z, 1 - c)
    right, far, left = (x + 1) % NX, (x + 2) % NX, (x + 3) % NX
    x_devs = [place((x + d) % NX, z, c) for d in (1, 2, 3)]
    z_devs = [place(x, (z + d) % NZ, c) for d in (1, 2, 3)]

    def rows_of(block):
        return pl.ds(pl.multiple_of(block * XROWS, XROWS), XROWS)

    own_cols = pl.ds(pl.multiple_of(c * width, BLOCK), width)
    oth_cols = pl.ds(pl.multiple_of((1 - c) * width, BLOCK), width)

    def local(src, dst, sem):
        pltpu.make_async_copy(src, dst, load_sem.at[sem]).start()

    def remote(src, dst, device, send, arrival):
        pltpu.make_async_remote_copy(
            src_ref=src, dst_ref=dst, send_sem=send_sem.at[send], recv_sem=recv_sem.at[arrival],
            device_id=device, device_id_type=MESH,
        ).start()

    def take(sem, ref):
        pltpu.make_async_copy(ref, ref, sem).wait()

    def loaded(sem, ref):
        take(load_sem.at[sem], ref)

    def arrived(sem, ref):
        take(recv_sem.at[sem], ref)

    def sent(sem, ref):
        take(send_sem.at[sem], ref)

    barrier = pltpu.get_barrier_semaphore()
    for device in x_devs + z_devs + [sibling]:
        pl.semaphore_signal(barrier, inc=1, device_id=device, device_id_type=MESH)

    order = (far, right, left, x)
    local(enc_exp, exp_words.at[0], EXPONENTS)
    local(ret_exp, exp_words.at[1], EXPONENTS)
    for which, block in enumerate(order):
        rows = rows_of(block)
        local(base.at[rows, own_cols], mine.at[0, rows], BLOCKS + which)
        local(params.at[0, rows, own_cols], mine.at[1, rows], BLOCKS + which)

    pl.semaphore_wait(barrier, 7)

    for which, block in enumerate(order):
        rows = rows_of(block)
        remote(params.at[0, rows, oth_cols], sib_params.at[rows], sibling, SWAP, IN_SWAP + which)
    moment_rows = pl.ds(pl.multiple_of(c * 8, 8), 8)
    other_rows = pl.ds(pl.multiple_of((1 - c) * 8, 8), 8)
    remote(momentum.at[:, oth_cols], moment.at[moment_rows], sibling, MOMENT, IN_MOMENT)
    pltpu.make_async_copy(momentum.at[:, own_cols], moment.at[moment_rows], recv_sem.at[IN_MOMENT]).start()
    local(base.at[:, oth_cols], oth_base, OTHER_BASE)

    loaded(EXPONENTS, exp_words)
    for half in range(2):
        for row in range(2):
            for tile in range(tiles):
                at = (half * 2 + row) * tiles + tile
                column = tile + (c if half == 0 else 1 - c) * tiles
                if half == 0:
                    exps[0, pl.ds(at, 1), :] = jnp.full((1, BLOCK), exp_words[0, row, column], jnp.int32)
                exps[1, pl.ds(at, 1), :] = jnp.full((1, BLOCK), exp_words[1, row, column], jnp.int32)
    encode_exps = exps[0, 0:2 * tiles, :]
    enc_mul[0:2 * tiles, :] = power_of_two(-encode_exps)
    later_tables = []

    def return_tables():
        if not later_tables:
            later_tables.append(True)
            return_exps = exps[1, 0:4 * tiles, :]
            enc_scale[0:2 * tiles, :] = power_of_two(exps[0, 0:2 * tiles, :]) * (1.0 / (2 * NX * NZ))
            ret_mul[0:4 * tiles, :] = power_of_two(-return_exps)
            ret_scale[0:4 * tiles, :] = power_of_two(return_exps)

    ready = set()

    def need(*blocks):
        for which in blocks:
            if which not in ready:
                ready.add(which)
                rows = rows_of(order[which])
                loaded(BLOCKS + which, mine.at[:, rows])
                arrived(IN_SWAP + which, sib_params.at[rows])

    def encoded_pair(which, tile):
        block = order[which]
        rows = rows_of(block)
        lanes = slice(tile * BLOCK, (tile + 1) * BLOCK)
        factor = enc_mul[pl.ds((block // 2) * tiles + tile, 1), :]
        start = mine[0, rows, lanes].astype(F32)
        total = None
        for source in (mine[1, rows, lanes], sib_params[rows, lanes]):
            code = jnp.clip((source.astype(F32) - start) * factor, -CODE_LIMIT, CODE_LIMIT)
            code = code.astype(BF16).astype(F32)
            total = code if total is None else total + code
        return total.reshape(NZ, ZROWS, BLOCK)

    def span(k):
        lo, hi, _ = CHUNKS[k]
        return range(lo, hi)

    def part(k):
        lo, hi, _ = CHUNKS[k]
        return pl.ds(lo, hi - lo)

    def mode(k):
        return CHUNKS[k][2]

    def event(k, what):
        return IN_CHUNKS + 9 * k + what

    def fill(which, k):
        for tile in span(k):
            shards[tile, order[which]] = encoded_pair(which, tile).astype(BF16)

    def encode(k):
        need(0, 1, 2)
        if mode(k) == ONE:
            for which, d in ((0, 2), (1, 1), (2, 3)):
                fill(which, k)
                remote(
                    shards.at[part(k), order[which]], x_in.at[d - 1, part(k)], x_devs[d - 1], SHARDS, event(k, FIRST)
                )
        else:
            need(3)
            for which in range(4):
                fill(which, k)
            for d in (2, 1, 3):
                remote(
                    shards.at[part(k), :, (z + d) % NZ], z_in.at[d - 1, part(k)], z_devs[d - 1], SHARDS, event(k, FIRST)
                )

    upper, lower = pl.ds(0, NZ // 2), pl.ds(NZ // 2, NZ // 2)

    def send_far(k):
        need(0)
        fill(0, k)
        remote(shards.at[part(k), far, upper], up_in.at[part(k)], x_devs[0], SHARDS, event(k, UP))
        remote(shards.at[part(k), far, lower], down_in.at[part(k)], x_devs[2], SHARDS, event(k, DOWN))

    def send_near(k):
        need(1, 2)
        fill(1, k)
        remote(shards.at[part(k), right, lower], x_in.at[0, part(k), lower], x_devs[0], SHARDS, event(k, FIRST))
        fill(2, k)
        remote(shards.at[part(k), left, upper], x_in.at[2, part(k), upper], x_devs[2], SHARDS, event(k, FIRST))

    def join(k):
        arrived(event(k, UP), up_in.at[part(k)])
        for tile in span(k):
            shards[tile, right, upper] = (shards[tile, right, upper].astype(F32) + up_in[tile].astype(F32)).astype(BF16)
        remote(shards.at[part(k), right, upper], x_in.at[0, part(k), upper], x_devs[0], SHARDS, event(k, FIRST))
        arrived(event(k, DOWN), down_in.at[part(k)])
        for tile in span(k):
            shards[tile, left, lower] = (shards[tile, left, lower].astype(F32) + down_in[tile].astype(F32)).astype(BF16)
        remote(shards.at[part(k), left, lower], x_in.at[2, part(k), lower], x_devs[2], SHARDS, event(k, FIRST))

    def sum_first(k):
        if mode(k) == ZFIRST:
            arrived(event(k, FIRST), z_in.at[:, part(k)])
        else:
            need(3)
            arrived(event(k, FIRST), x_in.at[pl.ds(0, 3 if mode(k) == ONE else 2), part(k)])
        for tile in span(k):
            if mode(k) == ZFIRST:
                total = shards[tile, :, z].astype(F32)
                parts = [z_in[d, tile] for d in range(3)]
            else:
                total = encoded_pair(3, tile)
                parts = [x_in[d, tile] for d in ((0, 1, 2) if mode(k) == ONE else (0, 2))]
            for piece in parts:
                total = total + piece.astype(F32)
            t_wide[tile] = total
            t_narrow[tile] = total.astype(BF16)
        for d in (2, 1, 3):
            if mode(k) == ZFIRST:
                remote(
                    t_narrow.at[part(k), (x + d) % NX], x_in.at[d - 1, part(k), 0], x_devs[d - 1], SUMS, event(k, SECOND)
                )
            else:
                remote(
                    t_narrow.at[part(k), (z + d) % NZ], z_in.at[d - 1, part(k), 0], z_devs[d - 1], SUMS, event(k, SECOND)
                )

    started = set()

    def step(k):
        return_tables()
        if not started:
            started.add(True)
            arrived(IN_MOMENT, moment)
        second = x_in if mode(k) == ZFIRST else z_in
        mine_at = x if mode(k) == ZFIRST else z
        arrived(event(k, SECOND), second.at[:, part(k), 0])
        for tile in span(k):
            lanes = slice(tile * BLOCK, (tile + 1) * BLOCK)
            at = pl.ds((x // 2) * tiles + tile, 1)
            summed = t_wide[tile, mine_at]
            for d in range(3):
                summed = summed + second[d, tile, 0].astype(F32)
            outer_grad = summed * enc_scale[at, :]
            new_moment = MOMENTUM_RATE * moment[:, lanes] + outer_grad
            moment_out[:, lanes] = new_moment
            outer_step = OUTER_RATE * (outer_grad + MOMENTUM_RATE * new_moment)
            code = jnp.clip(outer_step * ret_mul[at, :], -CODE_LIMIT, CODE_LIMIT)
            codes[tile, x, z] = code.astype(BF16)
        piece = codes.at[part(k), x, z]
        for d in (2, 1, 3):
            device = x_devs[d - 1] if mode(k) == ZFIRST else z_devs[d - 1]
            remote(piece, piece, device, CODES, event(k, CODES_IN))

    def to_sibling(k, block, arrival):
        remote(codes.at[part(k), block], sib_codes.at[part(k), block], sibling, CORE, event(k, arrival))

    def ring(k):
        arrived(event(k, CODES_IN), z_in.at[:, part(k), 0])
        if mode(k) == ZFIRST:
            piece = codes.at[part(k), :, z]
            for d in (2, 1, 3):
                remote(piece, piece, z_devs[d - 1], GATHER, event(k, FAR_IN))
        else:
            piece = codes.at[part(k), x]
            for d in (2, 1, 3):
                remote(piece, piece, x_devs[d - 1], GATHER, event(k, FAR_IN if d == 2 else NEAR_IN))
            to_sibling(k, x, CORE_NEAR)

    def land_near(k):
        arrived(event(k, NEAR_IN), codes.at[part(k), pl.ds(0, 2)])
        to_sibling(k, right, CORE_NEAR)
        to_sibling(k, left, CORE_NEAR)

    def land(k):
        if mode(k) == ZFIRST:
            arrived(event(k, FAR_IN), codes.at[part(k), pl.ds(0, 3)])
            remote(codes.at[part(k)], sib_codes.at[part(k)], sibling, CORE, event(k, CORE_FAR))
        else:
            arrived(event(k, FAR_IN), codes.at[part(k), 0])
            to_sibling(k, far, CORE_FAR)

    def apply(k, block, own):
        rows = rows_of(block)
        if not own and OTHER_BASE not in started:
            started.add(OTHER_BASE)
            loaded(OTHER_BASE, oth_base)
        for tile in span(k):
            lanes = slice(tile * BLOCK, (tile + 1) * BLOCK)
            at = pl.ds(((0 if own else 2) + block // 2) * tiles + tile, 1)
            code = (codes if own else sib_codes)[tile, block].reshape(XROWS, BLOCK).astype(F32)
            start = mine[0, rows, lanes] if own else oth_base[rows, lanes]
            out_lanes = pl.ds(pl.multiple_of((c if own else 1 - c) * width + tile * BLOCK, BLOCK), BLOCK)
            new_params[rows, out_lanes] = (start.astype(F32) + code * ret_scale[at, :]).astype(BF16)

    def own(k):
        apply(k, x, True)

    def own_near(k):
        apply(k, right, True)
        apply(k, left, True)

    def own_far(k):
        for block in order if mode(k) == ZFIRST else (far,):
            apply(k, block, True)

    def other_near(k):
        arrived(event(k, CORE_NEAR), codes.at[part(k), pl.ds(0, 3)])
        for block in (x, right, left):
            apply(k, block, False)

    def other_far(k):
        arrived(event(k, CORE_FAR), codes.at[part(k)] if mode(k) == ZFIRST else codes.at[part(k), 0])
        for block in order if mode(k) == ZFIRST else (far,):
            apply(k, block, False)

    stages = {
        ENCODE: encode, SEND_FAR: send_far, SEND_NEAR: send_near, JOIN: join, SUM: sum_first, STEP: step, RING: ring,
        LAND_NEAR: land_near, LAND: land, OWN: own, OWN_NEAR: own_near, OWN_FAR: own_far,
        OTHER_NEAR: other_near, OTHER_FAR: other_far,
    }
    steps_left = len(CHUNKS)
    for stage, k in SCHEDULE:
        stages[stage](k)
        if stage == STEP:
            steps_left -= 1
            if steps_left == 0:
                back = moment_out.at[other_rows]
                remote(back, new_momentum.at[:, own_cols], sibling, MOMENT, IN_MOMENT_BACK)
                new_momentum[:, own_cols] = moment_out[moment_rows]
    arrived(IN_MOMENT_BACK, new_momentum.at[:, oth_cols])

    sent(SWAP, sib_params)
    sent(SHARDS, shards.at[:, pl.ds(0, 3)])
    sent(SUMS, t_narrow.at[:, pl.ds(0, 3)])
    sent(CODES, t_narrow.at[:, pl.ds(0, 3)])
    sent(GATHER, codes.at[:, pl.ds(0, 3)])
    sent(CORE, codes)
    sent(MOMENT, moment)


def on_device(local_params, base_params, momentum, encode_exponents, return_exponents):
    _, rows, columns = local_params.shape
    width = columns // 2
    tiles = width // BLOCK
    table = pltpu.VMEM((-(-4 * tiles // 8) * 8, BLOCK), F32)
    half = pltpu.VMEM((rows, width), BF16)
    hbm = pl.BlockSpec(memory_space=pltpu.HBM)
    vmem = pl.BlockSpec(memory_space=pltpu.VMEM)
    return pl.pallas_call(
        kernel,
        name="outer_step",
        out_shape=(pltpu.VMEM((rows, columns), BF16), pltpu.VMEM(momentum.shape, F32)),
        in_specs=[hbm] * 5,
        out_specs=(vmem, vmem),
        scratch_shapes=[
            pltpu.SMEM((2,) + encode_exponents.shape, jnp.int32),
            pltpu.VMEM((2, rows, width), BF16),
            half, half,
            pltpu.VMEM((2, -(-4 * tiles // 8) * 8, BLOCK), jnp.int32),
            table, table, table, table,
            pltpu.VMEM((tiles, NX, NZ, ZROWS, BLOCK), BF16),
            pltpu.VMEM((tiles, NZ // 2, ZROWS, BLOCK), BF16),
            pltpu.VMEM((tiles, NZ // 2, ZROWS, BLOCK), BF16),
            pltpu.VMEM((3, tiles, NZ, ZROWS, BLOCK), BF16),
            pltpu.VMEM((3, tiles, NX, ZROWS, BLOCK), BF16),
            pltpu.VMEM((tiles, NZ, ZROWS, BLOCK), F32),
            pltpu.VMEM((tiles, NZ, ZROWS, BLOCK), BF16),
            pltpu.VMEM((ZROWS, width), F32),
            pltpu.VMEM((ZROWS, width), F32),
            pltpu.VMEM((tiles, NX, NZ, ZROWS, BLOCK), BF16),
            pltpu.VMEM((tiles, NX, NZ, ZROWS, BLOCK), BF16),
            pltpu.SemaphoreType.DMA((LOADS,)),
            pltpu.SemaphoreType.DMA((SENDS,)),
            pltpu.SemaphoreType.DMA((ARRIVALS,)),
        ],
        compiler_params=pltpu.CompilerParams(
            collective_id=0, has_side_effects=True, vmem_limit_bytes=32 * 2**20
        ),
        cost_estimate=pl.CostEstimate(flops=20_000_000, bytes_accessed=4_500_000, transcendentals=0),
    )(*[
        pltpu.with_memory_space_constraint(array, pltpu.HBM)
        for array in (local_params, base_params, momentum, encode_exponents, return_exponents)
    ])


def solution(mesh):
    return jax.shard_map(
        on_device,
        mesh=mesh,
        in_specs=(
            P("rep", None, "fsdp"),
            P(None, "fsdp"),
            P("rep", "fsdp"),
            P(None, "fsdp"),
            P(None, "fsdp"),
        ),
        out_specs=(P(None, "fsdp"), P("rep", "fsdp")),
        check_vma=False,
    )
```

time: 254 us -> 35.9 us (0.14)
  waiting for transfers between devices: 205 us -> 0 us
  Pallas kernels: 0 us -> 33.4 us
  local copies, waits for them, and re-layouts: 26.8 us -> 1.74 us
  between operations: 14.1 us -> 0.64 us
  other arithmetic: 7.84 us -> 0 us
    reduce_scatter x1 -> x0, waiting for transfers between devices: 140 us -> none  [sync_piece(): lax.psum_scatter(encoded.astype(jnp.float32), 'rep', scatter_dimension=0,...]
    all_gather x1 -> x0, waiting for transfers between devices: 64.8 us -> none  [sync_piece(): all_codes = lax.all_gather(delta_code, 'rep', axis=0, tiled=True)]
    pallas_call x0 -> x1, Pallas kernels: none -> 33.4 us  [on_device(): pl.pallas_call(kernel, name='outer_step', out_shape=(pltpu.VMEM((rows, co...]
    unnamed x18 -> x2, local copies, waits for them, and re-layouts: 18.2 us -> 1.74 us
    convert_element_type x3 -> x0, other arithmetic: 7.05 us -> none  [the longest x1 3.31 us: sync_piece(): (base_wide + all_codes.astype(jnp.float32) * scale_out).astype(jnp.bfloat16)]
    dynamic_slice x1 -> x0, local copies, waits for them, and re-layouts: 4.25 us -> none  [sync_piece(): own_out = lax.dynamic_slice_in_dim(scale_out, first_row, owned_rows, 0)]
  transfers between devices with their start and end apart: 2 -> 0, of which waited for: 2 -> 0; matrix products, arithmetic and copies ran while one was open for 5% -> 0% of each run, Pallas kernels for 0% -> 0%
where the time goes in v3:
time: 35.9 us; the launch traced here: 35.8 us
  Pallas kernels  33.4 us (93%)
  local copies, waits for them, and re-layouts  1.74 us (5%)
  between operations  0.64 us (2%)
    pallas_call x1, Pallas kernels, on_device(): pl.pallas_call(kernel, name='outer_step', out_shape=(pltpu.VMEM((rows, co...  33.4 us
    unnamed x2, local copies, waits for them, and re-layouts  1.74 us

profile of v3, /device:TPU:1, one launch (start us, length us, event | category | flops | bytes accessed | tf_op | source)
XLA Modules:
  0.0 35.8 jit_solution(6678367844692466499)
XLA Ops:
  0.6 33.4 %outer_step.1 = (bf16[256,2816]{1,0:T(8,128)(2,1)S(1)}, f32[8,2816]{1,0:T(8,128)S(1)}) custom-call(bf16[1,256,2816]{2,1,0:T(8,128)(2,1)} %params.1, bf16[256,2816]{1,0:T(8,128)(2,1)} %base.1, f32[8,2816]{1,0:T(8,128)} %momentum.1, s32[2,22]{1,0:T(2,128)} %enc_exp.1, s32[2,22]{1,0:T(2,128)} %ret_exp.1), custom_call_target="tpu_custom_call" | custom-call | flops 20000000 | bytes 4500000 | tf_op jit(solution)/shard_map/outer_step/pallas_call | solution.py:373
  34.0 1.1 %copy.9 = bf16[256,2816]{1,0:T(8,128)(2,1)} copy(bf16[256,2816]{1,0:T(8,128)(2,1)S(1)} %get-tuple-element.2) | data formatting | bytes 2883584
  35.1 0.6 %copy.10 = f32[8,2816]{1,0:T(8,128)} copy(f32[8,2816]{1,0:T(8,128)S(1)} %get-tuple-element.3) | data formatting | bytes 180224

commit v4 on v3

--- a/solution.py
+++ b/solution.py
@@ -16,25 +16,41 @@
 XROWS = NZ * ZROWS
 
 ONE, TWO, ZFIRST = range(3)
-CHUNKS = ((0, 3, ONE), (3, 6, ONE), (6, 9, TWO), (9, 11, ZFIRST))
+CHUNKS = ((0, 4, TWO, ONE), (4, 8, TWO, ONE), (8, 11, ZFIRST, ONE))
 BLOCKS, EXPONENTS, OTHER_BASE = 0, 4, 5
 LOADS = 6
 SWAP, SHARDS, SUMS, CODES, GATHER, CORE, MOMENT = range(7)
 SENDS = 7
 IN_SWAP, IN_MOMENT, IN_MOMENT_BACK, IN_CHUNKS = 0, 4, 5, 6
-UP, DOWN, FIRST, SECOND, CODES_IN, NEAR_IN, FAR_IN, CORE_NEAR, CORE_FAR = range(9)
-ARRIVALS = IN_CHUNKS + 9 * len(CHUNKS)
-ENCODE, SEND_FAR, SEND_NEAR, JOIN, SUM, STEP, RING, LAND_NEAR, LAND, OWN, OWN_NEAR, OWN_FAR, OTHER_NEAR, OTHER_FAR = range(14)
+FIRST, SECOND, CODES_IN, FAR_IN, CORE_FAR, NEAR_IN, CORE_NEAR, UP, DOWN, RIGHTWARD, LEFTWARD = range(11)
+
+
+def events():
+    table = {}
+    for k, (_, _, how, gather) in enumerate(CHUNKS):
+        kinds = [FIRST, SECOND, CODES_IN, FAR_IN, CORE_FAR]
+        kinds += [] if how == ZFIRST else [NEAR_IN, CORE_NEAR]
+        kinds += [UP, DOWN] if how == TWO else []
+        kinds += [RIGHTWARD, LEFTWARD] if gather == TWO else []
+        for kind in kinds:
+            table[k, kind] = IN_CHUNKS + len(table)
+    return table
+
+
+EVENTS = events()
+ARRIVALS = IN_CHUNKS + len(EVENTS)
+(
+    ENCODE, SEND_FAR, SEND_NEAR, JOIN, PAIR, SUM, STEP, RING, PASS, LAND_NEAR, LAND,
+    OWN, OWN_NEAR, OWN_FAR, OTHER_NEAR, OTHER_FAR,
+) = range(16)
 SCHEDULE = (
-    (SEND_FAR, 2), (ENCODE, 0), (ENCODE, 1), (SEND_NEAR, 2), (ENCODE, 3),
-    (JOIN, 2), (SUM, 0), (SUM, 1), (SUM, 3), (SUM, 2),
-    (STEP, 0), (STEP, 3), (STEP, 1), (STEP, 2), (RING, 0),
-    (OWN, 0), (RING, 3), (RING, 1), (OWN, 1), (RING, 2),
-    (OWN, 2), (LAND, 0), (OWN_FAR, 0), (LAND_NEAR, 0), (OWN_NEAR, 0),
-    (OTHER_FAR, 0), (OTHER_NEAR, 0), (LAND, 1), (OWN_FAR, 1), (LAND_NEAR, 1),
-    (LAND, 3), (OWN_NEAR, 1), (OWN_FAR, 3), (OTHER_FAR, 1), (OTHER_NEAR, 1),
-    (OTHER_FAR, 3), (LAND, 2), (OWN_FAR, 2), (LAND_NEAR, 2), (OWN_NEAR, 2),
-    (OTHER_FAR, 2), (OTHER_NEAR, 2),
+    (SEND_FAR, 0), (SEND_FAR, 1), (SEND_NEAR, 0), (SEND_NEAR, 1), (ENCODE, 2),
+    (PAIR, 0), (PAIR, 1), (JOIN, 0), (JOIN, 1), (SUM, 0),
+    (SUM, 1), (SUM, 2), (STEP, 0), (STEP, 2), (STEP, 1),
+    (RING, 2), (RING, 0), (OWN, 0), (RING, 1), (OWN, 1),
+    (LAND, 0), (OWN_FAR, 0), (LAND_NEAR, 0), (OWN_NEAR, 0), (OTHER_FAR, 0),
+    (OTHER_NEAR, 0), (LAND, 1), (OWN_FAR, 1), (LAND, 2), (OWN_FAR, 2),
+    (LAND_NEAR, 1), (OWN_NEAR, 1), (OTHER_FAR, 1), (OTHER_FAR, 2), (OTHER_NEAR, 1),
 )
 
 
@@ -162,18 +178,18 @@
         return total.reshape(NZ, ZROWS, BLOCK)
 
     def span(k):
-        lo, hi, _ = CHUNKS[k]
+        lo, hi = CHUNKS[k][:2]
         return range(lo, hi)
 
     def part(k):
-        lo, hi, _ = CHUNKS[k]
+        lo, hi = CHUNKS[k][:2]
         return pl.ds(lo, hi - lo)
 
     def mode(k):
         return CHUNKS[k][2]
 
     def event(k, what):
-        return IN_CHUNKS + 9 * k + what
+        return EVENTS[k, what]
 
     def fill(which, k):
         for tile in span(k):
@@ -221,18 +237,22 @@
             shards[tile, left, lower] = (shards[tile, left, lower].astype(F32) + down_in[tile].astype(F32)).astype(BF16)
         remote(shards.at[part(k), left, lower], x_in.at[2, part(k), lower], x_devs[2], SHARDS, event(k, FIRST))
 
+    def pair(k):
+        need(3)
+        for tile in span(k):
+            t_wide[tile] = encoded_pair(3, tile)
+
     def sum_first(k):
         if mode(k) == ZFIRST:
             arrived(event(k, FIRST), z_in.at[:, part(k)])
         else:
-            need(3)
             arrived(event(k, FIRST), x_in.at[pl.ds(0, 3 if mode(k) == ONE else 2), part(k)])
         for tile in span(k):
             if mode(k) == ZFIRST:
                 total = shards[tile, :, z].astype(F32)
                 parts = [z_in[d, tile] for d in range(3)]
             else:
-                total = encoded_pair(3, tile)
+                total = t_wide[tile]
                 parts = [x_in[d, tile] for d in ((0, 1, 2) if mode(k) == ONE else (0, 2))]
             for piece in parts:
                 total = total + piece.astype(F32)
@@ -284,14 +304,28 @@
             piece = codes.at[part(k), :, z]
             for d in (2, 1, 3):
                 remote(piece, piece, z_devs[d - 1], GATHER, event(k, FAR_IN))
-        else:
+        elif CHUNKS[k][3] == ONE:
             piece = codes.at[part(k), x]
             for d in (2, 1, 3):
                 remote(piece, piece, x_devs[d - 1], GATHER, event(k, FAR_IN if d == 2 else NEAR_IN))
             to_sibling(k, x, CORE_NEAR)
+        else:
+            first, second = codes.at[part(k), x, upper], codes.at[part(k), x, lower]
+            remote(first, first, x_devs[0], GATHER, event(k, RIGHTWARD))
+            remote(second, second, x_devs[2], GATHER, event(k, LEFTWARD))
+            remote(second, second, x_devs[0], GATHER, event(k, NEAR_IN))
+            remote(first, first, x_devs[2], GATHER, event(k, NEAR_IN))
+            to_sibling(k, x, CORE_NEAR)
+
+    def pass_on(k):
+        first, second = codes.at[part(k), left, upper], codes.at[part(k), right, lower]
+        arrived(event(k, RIGHTWARD), first)
+        remote(first, first, x_devs[0], GATHER, event(k, FAR_IN))
+        arrived(event(k, LEFTWARD), second)
+        remote(second, second, x_devs[2], GATHER, event(k, FAR_IN))
 
     def land_near(k):
-        arrived(event(k, NEAR_IN), codes.at[part(k), pl.ds(0, 2)])
+        arrived(event(k, NEAR_IN), codes.at[part(k), pl.ds(0, 2 if CHUNKS[k][3] == ONE else 1)])
         to_sibling(k, right, CORE_NEAR)
         to_sibling(k, left, CORE_NEAR)
 
@@ -338,7 +372,8 @@
             apply(k, block, False)
 
     stages = {
-        ENCODE: encode, SEND_FAR: send_far, SEND_NEAR: send_near, JOIN: join, SUM: sum_first, STEP: step, RING: ring,
+        ENCODE: encode, SEND_FAR: send_far, SEND_NEAR: send_near, JOIN: join, PAIR: pair, SUM: sum_first,
+        STEP: step, RING: ring, PASS: pass_on,
         LAND_NEAR: land_near, LAND: land, OWN: own, OWN_NEAR: own_near, OWN_FAR: own_far,
         OTHER_NEAR: other_near, OTHER_FAR: other_far,
     }
@@ -362,6 +397,16 @@
     sent(MOMENT, moment)
 
 
+def store(params, momentum, params_out, momentum_out, sem):
+    copies = [
+        pltpu.make_async_copy(params, params_out, sem.at[0]), pltpu.make_async_copy(momentum, momentum_out, sem.at[1])
+    ]
+    for copy in copies:
+        copy.start()
+    for copy in copies:
+        copy.wait()
+
+
 def on_device(local_params, base_params, momentum, encode_exponents, return_exponents):
     _, rows, columns = local_params.shape
     width = columns // 2
@@ -370,7 +415,7 @@
     half = pltpu.VMEM((rows, width), BF16)
     hbm = pl.BlockSpec(memory_space=pltpu.HBM)
     vmem = pl.BlockSpec(memory_space=pltpu.VMEM)
-    return pl.pallas_call(
+    held = pl.pallas_call(
         kernel,
         name="outer_step",
         out_shape=(pltpu.VMEM((rows, columns), BF16), pltpu.VMEM(momentum.shape, F32)),
@@ -405,6 +450,14 @@
         pltpu.with_memory_space_constraint(array, pltpu.HBM)
         for array in (local_params, base_params, momentum, encode_exponents, return_exponents)
     ])
+    return pl.pallas_call(
+        store,
+        name="store",
+        out_shape=tuple(pltpu.HBM(array.shape, array.dtype) for array in held),
+        in_specs=[vmem, vmem],
+        out_specs=(hbm, hbm),
+        scratch_shapes=[pltpu.SemaphoreType.DMA((2,))],
+    )(*[pltpu.with_memory_space_constraint(array, pltpu.VMEM) for array in held])
 
 
 def solution(mesh):

time: 35.9 us -> 35.4 us (0.986)
  local copies, waits for them, and re-layouts: 1.74 us -> 0 us
  Pallas kernels: 33.4 us -> 34.6 us
    unnamed x2 -> x0, local copies, waits for them, and re-layouts: 1.74 us -> none
    pallas_call x0 -> x1, Pallas kernels: none -> 1.13 us  [on_device(): pl.pallas_call(store, name='store', out_shape=tuple((pltpu.HBM(array.shap...]
where the time goes in v4:
time: 35.4 us; the launch traced here: 35.2 us
  Pallas kernels  34.6 us (98%)
  between operations  0.64 us (2%)
    pallas_call x1, Pallas kernels, on_device(): pl.pallas_call(kernel, name='outer_step', out_shape=(pltpu.VMEM((rows, co...  33.5 us
    pallas_call x1, Pallas kernels, on_device(): pl.pallas_call(store, name='store', out_shape=tuple((pltpu.HBM(array.shap...  1.13 us

profile of v4, /device:TPU:1, one launch (start us, length us, event | category | flops | bytes accessed | tf_op | source)
XLA Modules:
  0.0 35.2 jit_solution(10091880181711812945)
XLA Ops:
  0.6 33.5 %outer_step.1 = (bf16[256,2816]{1,0:T(8,128)(2,1)S(1)}, f32[8,2816]{1,0:T(8,128)S(1)}) custom-call(bf16[1,256,2816]{2,1,0:T(8,128)(2,1)} %params.1, bf16[256,2816]{1,0:T(8,128)(2,1)} %base.1, f32[8,2816]{1,0:T(8,128)} %momentum.1, s32[2,22]{1,0:T(2,128)} %enc_exp.1, s32[2,22]{1,0:T(2,128)} %ret_exp.1), custom_call_target="tpu_custom_call" | custom-call | flops 20000000 | bytes 4500000 | tf_op jit(solution)/shard_map/outer_step/pallas_call | solution.py:418
  34.1 1.1 %store.1 = (bf16[256,2816]{1,0:T(8,128)(2,1)}, f32[8,2816]{1,0:T(8,128)}) custom-call(bf16[256,2816]{1,0:T(8,128)(2,1)S(1)} %get-tuple-element.4.params, f32[8,2816]{1,0:T(8,128)S(1)} %get-tuple-element.5.momentum), custom_call_target="tpu_custom_call" | custom-call | tf_op jit(solution)/shard_map/store/pallas_call | solution.py:453

commit v5 on v3

--- a/solution.py
+++ b/solution.py
@@ -15,26 +15,41 @@
 ZROWS = 16
 XROWS = NZ * ZROWS
 
-ONE, TWO, ZFIRST = range(3)
-CHUNKS = ((0, 3, ONE), (3, 6, ONE), (6, 9, TWO), (9, 11, ZFIRST))
-BLOCKS, EXPONENTS, OTHER_BASE = 0, 4, 5
-LOADS = 6
+ONE, ZFIRST = range(2)
+CHUNKS = ((0, 2, ONE), (2, 5, ONE), (5, 8, ONE), (8, 10, ZFIRST), (10, 11, ZFIRST))
+BLOCKS, EXPONENTS, OTHER_BASE = 0, 5, 6
+LOADS = 7
 SWAP, SHARDS, SUMS, CODES, GATHER, CORE, MOMENT = range(7)
 SENDS = 7
-IN_SWAP, IN_MOMENT, IN_MOMENT_BACK, IN_CHUNKS = 0, 4, 5, 6
-UP, DOWN, FIRST, SECOND, CODES_IN, NEAR_IN, FAR_IN, CORE_NEAR, CORE_FAR = range(9)
-ARRIVALS = IN_CHUNKS + 9 * len(CHUNKS)
-ENCODE, SEND_FAR, SEND_NEAR, JOIN, SUM, STEP, RING, LAND_NEAR, LAND, OWN, OWN_NEAR, OWN_FAR, OTHER_NEAR, OTHER_FAR = range(14)
+IN_SWAP, IN_MOMENT, IN_MOMENT_BACK, IN_CHUNKS = 0, 5, 6, 7
+Z_TILE = min([lo for lo, _, how in CHUNKS if how == ZFIRST], default=0)
+WHOLE = 4
+FIRST, OWNED, SECOND, FAR_IN, CORE_FAR, CODES_IN, NEAR_IN, CORE_NEAR = 0, 1, 2, 3, 4, 5, 9, 10
+
+
+def chunk_starts():
+    starts = [IN_CHUNKS]
+    for _, _, how in CHUNKS:
+        starts.append(starts[-1] + (9 if how == ZFIRST else 11))
+    return starts
+
+
+STARTS = chunk_starts()
+ARRIVALS = STARTS[-1]
+(
+    ENCODE, SEND_OWNED, PAIR, SUM, STEP, RING, LAND_NEAR, LAND, OWN, OWN_NEAR, OWN_FAR, OTHER_NEAR, OTHER_FAR,
+) = range(13)
 SCHEDULE = (
-    (SEND_FAR, 2), (ENCODE, 0), (ENCODE, 1), (SEND_NEAR, 2), (ENCODE, 3),
-    (JOIN, 2), (SUM, 0), (SUM, 1), (SUM, 3), (SUM, 2),
-    (STEP, 0), (STEP, 3), (STEP, 1), (STEP, 2), (RING, 0),
-    (OWN, 0), (RING, 3), (RING, 1), (OWN, 1), (RING, 2),
-    (OWN, 2), (LAND, 0), (OWN_FAR, 0), (LAND_NEAR, 0), (OWN_NEAR, 0),
-    (OTHER_FAR, 0), (OTHER_NEAR, 0), (LAND, 1), (OWN_FAR, 1), (LAND_NEAR, 1),
-    (LAND, 3), (OWN_NEAR, 1), (OWN_FAR, 3), (OTHER_FAR, 1), (OTHER_NEAR, 1),
-    (OTHER_FAR, 3), (LAND, 2), (OWN_FAR, 2), (LAND_NEAR, 2), (OWN_NEAR, 2),
-    (OTHER_FAR, 2), (OTHER_NEAR, 2),
+    (ENCODE, 0), (ENCODE, 1), (ENCODE, 2), (PAIR, 0), (PAIR, 1), (PAIR, 2),
+    (ENCODE, 3), (ENCODE, 4), (SEND_OWNED, 0), (SEND_OWNED, 1), (SEND_OWNED, 2), (SEND_OWNED, 3),
+    (SEND_OWNED, 4), (SUM, 0), (SUM, 1), (SUM, 3), (SUM, 2), (SUM, 4),
+    (STEP, 0), (STEP, 1), (STEP, 3), (STEP, 4), (STEP, 2), (RING, 0),
+    (OWN, 0), (RING, 3), (RING, 4), (RING, 1), (OWN, 1), (RING, 2),
+    (OWN, 2), (LAND_NEAR, 0), (OWN_NEAR, 0), (LAND, 0), (OWN_FAR, 0), (OTHER_NEAR, 0),
+    (OTHER_FAR, 0), (LAND_NEAR, 1), (LAND, 1), (OWN_NEAR, 1), (OWN_FAR, 1), (LAND, 3),
+    (OWN_FAR, 3), (OTHER_NEAR, 1), (OTHER_FAR, 1), (LAND_NEAR, 2), (LAND, 2), (OWN_NEAR, 2),
+    (LAND, 4), (OWN_FAR, 2), (OWN_FAR, 4), (OTHER_FAR, 3), (OTHER_NEAR, 2), (OTHER_FAR, 2),
+    (OTHER_FAR, 4),
 )
 
 
@@ -51,7 +66,7 @@
 def kernel(
     params, base, momentum, enc_exp, ret_exp, new_params, new_momentum,
     exp_words, mine, sib_params, oth_base, exps, enc_mul, enc_scale, ret_mul, ret_scale,
-    shards, up_in, down_in, x_in, z_in, t_wide, t_narrow, moment, moment_out, codes, sib_codes,
+    shards, x_in, z_in, t_wide, t_narrow, moment, moment_out, codes, sib_codes,
     load_sem, send_sem, recv_sem,
 ):
     rep = lax.axis_index("rep")
@@ -99,18 +114,33 @@
         pl.semaphore_signal(barrier, inc=1, device_id=device, device_id_type=MESH)
 
     order = (far, right, left, x)
+    first_z = Z_TILE * BLOCK
+
+    def piece(which):
+        if which == WHOLE:
+            return pl.ds(0, NX * XROWS), first_z, width - first_z
+        return rows_of(order[which]), 0, first_z
+
+    def columns(core, first, count):
+        return pl.ds(pl.multiple_of(core * width + first, BLOCK), count)
+
+    pieces = (0, 1, 2, 3, WHOLE)
+    for which in pieces:
+        rows, first, count = piece(which)
+        lanes = pl.ds(first, count)
+        local(base.at[rows, columns(c, first, count)], mine.at[0, rows, lanes], BLOCKS + which)
+        local(params.at[0, rows, columns(c, first, count)], mine.at[1, rows, lanes], BLOCKS + which)
     local(enc_exp, exp_words.at[0], EXPONENTS)
     local(ret_exp, exp_words.at[1], EXPONENTS)
-    for which, block in enumerate(order):
-        rows = rows_of(block)
-        local(base.at[rows, own_cols], mine.at[0, rows], BLOCKS + which)
-        local(params.at[0, rows, own_cols], mine.at[1, rows], BLOCKS + which)
 
     pl.semaphore_wait(barrier, 7)
 
-    for which, block in enumerate(order):
-        rows = rows_of(block)
-        remote(params.at[0, rows, oth_cols], sib_params.at[rows], sibling, SWAP, IN_SWAP + which)
+    for which in pieces:
+        rows, first, count = piece(which)
+        remote(
+            params.at[0, rows, columns(1 - c, first, count)], sib_params.at[rows, pl.ds(first, count)],
+            sibling, SWAP, IN_SWAP + which,
+        )
     moment_rows = pl.ds(pl.multiple_of(c * 8, 8), 8)
     other_rows = pl.ds(pl.multiple_of((1 - c) * 8, 8), 8)
     remote(momentum.at[:, oth_cols], moment.at[moment_rows], sibling, MOMENT, IN_MOMENT)
@@ -144,9 +174,10 @@
         for which in blocks:
             if which not in ready:
                 ready.add(which)
-                rows = rows_of(order[which])
-                loaded(BLOCKS + which, mine.at[:, rows])
-                arrived(IN_SWAP + which, sib_params.at[rows])
+                rows, first, count = piece(which)
+                lanes = pl.ds(first, count)
+                loaded(BLOCKS + which, mine.at[:, rows, lanes])
+                arrived(IN_SWAP + which, sib_params.at[rows, lanes])
 
     def encoded_pair(which, tile):
         block = order[which]
@@ -162,91 +193,81 @@
         return total.reshape(NZ, ZROWS, BLOCK)
 
     def span(k):
-        lo, hi, _ = CHUNKS[k]
+        lo, hi = CHUNKS[k][:2]
         return range(lo, hi)
 
     def part(k):
-        lo, hi, _ = CHUNKS[k]
+        lo, hi = CHUNKS[k][:2]
         return pl.ds(lo, hi - lo)
 
     def mode(k):
         return CHUNKS[k][2]
 
     def event(k, what):
-        return IN_CHUNKS + 9 * k + what
+        return STARTS[k] + what
 
     def fill(which, k):
         for tile in span(k):
             shards[tile, order[which]] = encoded_pair(which, tile).astype(BF16)
 
     def encode(k):
-        need(0, 1, 2)
         if mode(k) == ONE:
+            need(0, 1, 2)
             for which, d in ((0, 2), (1, 1), (2, 3)):
                 fill(which, k)
-                remote(
-                    shards.at[part(k), order[which]], x_in.at[d - 1, part(k)], x_devs[d - 1], SHARDS, event(k, FIRST)
-                )
+                for e in (2, 1, 3):
+                    at = (z + e) % NZ
+                    remote(
+                        shards.at[part(k), order[which], at], x_in.at[d - 1, part(k), at], x_devs[d - 1],
+                        SHARDS, event(k, FIRST),
+                    )
         else:
-            need(3)
+            need(WHOLE)
             for which in range(4):
                 fill(which, k)
             for d in (2, 1, 3):
+                for e in (2, 1, 3):
+                    at = (x + e) % NX
+                    remote(
+                        shards.at[part(k), at, (z + d) % NZ], z_in.at[d - 1, part(k), at], z_devs[d - 1],
+                        SHARDS, event(k, FIRST),
+                    )
+
+    def send_owned(k):
+        for d in (2, 1, 3):
+            if mode(k) == ONE:
                 remote(
-                    shards.at[part(k), :, (z + d) % NZ], z_in.at[d - 1, part(k)], z_devs[d - 1], SHARDS, event(k, FIRST)
-                )
-
-    upper, lower = pl.ds(0, NZ // 2), pl.ds(NZ // 2, NZ // 2)
-
-    def send_far(k):
-        need(0)
-        fill(0, k)
-        remote(shards.at[part(k), far, upper], up_in.at[part(k)], x_devs[0], SHARDS, event(k, UP))
-        remote(shards.at[part(k), far, lower], down_in.at[part(k)], x_devs[2], SHARDS, event(k, DOWN))
-
-    def send_near(k):
-        need(1, 2)
-        fill(1, k)
-        remote(shards.at[part(k), right, lower], x_in.at[0, part(k), lower], x_devs[0], SHARDS, event(k, FIRST))
-        fill(2, k)
-        remote(shards.at[part(k), left, upper], x_in.at[2, part(k), upper], x_devs[2], SHARDS, event(k, FIRST))
-
-    def join(k):
-        arrived(event(k, UP), up_in.at[part(k)])
-        for tile in span(k):
-            shards[tile, right, upper] = (shards[tile, right, upper].astype(F32) + up_in[tile].astype(F32)).astype(BF16)
-        remote(shards.at[part(k), right, upper], x_in.at[0, part(k), upper], x_devs[0], SHARDS, event(k, FIRST))
-        arrived(event(k, DOWN), down_in.at[part(k)])
-        for tile in span(k):
-            shards[tile, left, lower] = (shards[tile, left, lower].astype(F32) + down_in[tile].astype(F32)).astype(BF16)
-        remote(shards.at[part(k), left, lower], x_in.at[2, part(k), lower], x_devs[2], SHARDS, event(k, FIRST))
-
-    def sum_first(k):
-        if mode(k) == ZFIRST:
-            arrived(event(k, FIRST), z_in.at[:, part(k)])
-        else:
-            need(3)
-            arrived(event(k, FIRST), x_in.at[pl.ds(0, 3 if mode(k) == ONE else 2), part(k)])
-        for tile in span(k):
-            if mode(k) == ZFIRST:
-                total = shards[tile, :, z].astype(F32)
-                parts = [z_in[d, tile] for d in range(3)]
-            else:
-                total = encoded_pair(3, tile)
-                parts = [x_in[d, tile] for d in ((0, 1, 2) if mode(k) == ONE else (0, 2))]
-            for piece in parts:
-                total = total + piece.astype(F32)
-            t_wide[tile] = total
-            t_narrow[tile] = total.astype(BF16)
-        for d in (2, 1, 3):
-            if mode(k) == ZFIRST:
-                remote(
-                    t_narrow.at[part(k), (x + d) % NX], x_in.at[d - 1, part(k), 0], x_devs[d - 1], SUMS, event(k, SECOND)
+                    shards.at[part(k), (x + d) % NX, z], x_in.at[d - 1, part(k), z], x_devs[d - 1],
+                    SHARDS, event(k, OWNED),
                 )
             else:
                 remote(
-                    t_narrow.at[part(k), (z + d) % NZ], z_in.at[d - 1, part(k), 0], z_devs[d - 1], SUMS, event(k, SECOND)
+                    shards.at[part(k), x, (z + d) % NZ], z_in.at[d - 1, part(k), x], z_devs[d - 1],
+                    SHARDS, event(k, OWNED),
                 )
+
+    def pair(k):
+        need(3)
+        for tile in span(k):
+            t_wide[tile] = encoded_pair(3, tile)
+
+    def first_total(k, tile, at):
+        if mode(k) == ONE:
+            total, parts = t_wide[tile, at], x_in
+        else:
+            total, parts = shards[tile, at, z].astype(F32), z_in
+        for d in range(3):
+            total = total + parts[d, tile, at].astype(F32)
+        return total
+
+    def sum_first(k):
+        arrived(event(k, FIRST), (x_in if mode(k) == ONE else z_in).at[:, part(k), pl.ds(0, 3)])
+        for d in (2, 1, 3):
+            at = ((z if mode(k) == ONE else x) + d) % NZ
+            for tile in span(k):
+                t_narrow[tile, at] = first_total(k, tile, at).astype(BF16)
+            landing, devices = (z_in, z_devs) if mode(k) == ONE else (x_in, x_devs)
+            remote(t_narrow.at[part(k), at], landing.at[d - 1, part(k), 0], devices[d - 1], SUMS, event(k, SECOND))
 
     started = set()
 
@@ -257,11 +278,12 @@
             arrived(IN_MOMENT, moment)
         second = x_in if mode(k) == ZFIRST else z_in
         mine_at = x if mode(k) == ZFIRST else z
+        arrived(event(k, OWNED), second.at[:, part(k), 0])
         arrived(event(k, SECOND), second.at[:, part(k), 0])
         for tile in span(k):
             lanes = slice(tile * BLOCK, (tile + 1) * BLOCK)
             at = pl.ds((x // 2) * tiles + tile, 1)
-            summed = t_wide[tile, mine_at]
+            summed = first_total(k, tile, mine_at)
             for d in range(3):
                 summed = summed + second[d, tile, 0].astype(F32)
             outer_grad = summed * enc_scale[at, :]
@@ -272,22 +294,30 @@
             codes[tile, x, z] = code.astype(BF16)
         piece = codes.at[part(k), x, z]
         for d in (2, 1, 3):
-            device = x_devs[d - 1] if mode(k) == ZFIRST else z_devs[d - 1]
-            remote(piece, piece, device, CODES, event(k, CODES_IN))
+            if mode(k) == ONE:
+                remote(piece, piece, z_devs[d - 1], CODES, event(k, CODES_IN + z))
+            else:
+                remote(piece, piece, x_devs[d - 1], CODES, event(k, CODES_IN + x))
+        gather(k, piece)
+
+    def gather(k, piece):
+        for d in (2, 1, 3):
+            if mode(k) == ONE:
+                remote(piece, piece, x_devs[d - 1], GATHER, event(k, FAR_IN if d == 2 else NEAR_IN))
+            else:
+                remote(piece, piece, z_devs[d - 1], GATHER, event(k, FAR_IN))
 
     def to_sibling(k, block, arrival):
         remote(codes.at[part(k), block], sib_codes.at[part(k), block], sibling, CORE, event(k, arrival))
 
+    line_order = [jnp.where(z < 2, at, 3 - at) for at in (1 - jnp.minimum(z, 3 - z), 2, 3)]
+
     def ring(k):
-        arrived(event(k, CODES_IN), z_in.at[:, part(k), 0])
-        if mode(k) == ZFIRST:
-            piece = codes.at[part(k), :, z]
-            for d in (2, 1, 3):
-                remote(piece, piece, z_devs[d - 1], GATHER, event(k, FAR_IN))
-        else:
-            piece = codes.at[part(k), x]
-            for d in (2, 1, 3):
-                remote(piece, piece, x_devs[d - 1], GATHER, event(k, FAR_IN if d == 2 else NEAR_IN))
+        for at in line_order if mode(k) == ONE else (right, left, far):
+            piece = codes.at[part(k), x, at] if mode(k) == ONE else codes.at[part(k), at, z]
+            arrived(event(k, CODES_IN + at), piece)
+            gather(k, piece)
+        if mode(k) == ONE:
             to_sibling(k, x, CORE_NEAR)
 
     def land_near(k):
@@ -338,7 +368,7 @@
             apply(k, block, False)
 
     stages = {
-        ENCODE: encode, SEND_FAR: send_far, SEND_NEAR: send_near, JOIN: join, SUM: sum_first, STEP: step, RING: ring,
+        ENCODE: encode, SEND_OWNED: send_owned, PAIR: pair, SUM: sum_first, STEP: step, RING: ring,
         LAND_NEAR: land_near, LAND: land, OWN: own, OWN_NEAR: own_near, OWN_FAR: own_far,
         OTHER_NEAR: other_near, OTHER_FAR: other_far,
     }
@@ -362,6 +392,16 @@
     sent(MOMENT, moment)
 
 
+def store(params, momentum, params_out, momentum_out, sem):
+    copies = [
+        pltpu.make_async_copy(params, params_out, sem.at[0]), pltpu.make_async_copy(momentum, momentum_out, sem.at[1])
+    ]
+    for copy in copies:
+        copy.start()
+    for copy in copies:
+        copy.wait()
+
+
 def on_device(local_params, base_params, momentum, encode_exponents, return_exponents):
     _, rows, columns = local_params.shape
     width = columns // 2
@@ -370,7 +410,7 @@
     half = pltpu.VMEM((rows, width), BF16)
     hbm = pl.BlockSpec(memory_space=pltpu.HBM)
     vmem = pl.BlockSpec(memory_space=pltpu.VMEM)
-    return pl.pallas_call(
+    held = pl.pallas_call(
         kernel,
         name="outer_step",
         out_shape=(pltpu.VMEM((rows, columns), BF16), pltpu.VMEM(momentum.shape, F32)),
@@ -383,8 +423,6 @@
             pltpu.VMEM((2, -(-4 * tiles // 8) * 8, BLOCK), jnp.int32),
             table, table, table, table,
             pltpu.VMEM((tiles, NX, NZ, ZROWS, BLOCK), BF16),
-            pltpu.VMEM((tiles, NZ // 2, ZROWS, BLOCK), BF16),
-            pltpu.VMEM((tiles, NZ // 2, ZROWS, BLOCK), BF16),
             pltpu.VMEM((3, tiles, NZ, ZROWS, BLOCK), BF16),
             pltpu.VMEM((3, tiles, NX, ZROWS, BLOCK), BF16),
             pltpu.VMEM((tiles, NZ, ZROWS, BLOCK), F32),
@@ -405,6 +443,14 @@
         pltpu.with_memory_space_constraint(array, pltpu.HBM)
         for array in (local_params, base_params, momentum, encode_exponents, return_exponents)
     ])
+    return pl.pallas_call(
+        store,
+        name="store",
+        out_shape=tuple(pltpu.HBM(array.shape, array.dtype) for array in held),
+        in_specs=[vmem, vmem],
+        out_specs=(hbm, hbm),
+        scratch_shapes=[pltpu.SemaphoreType.DMA((2,))],
+    )(*[pltpu.with_memory_space_constraint(array, pltpu.VMEM) for array in held])
 
 
 def solution(mesh):

time: 35.9 us -> 32.8 us (0.914)
  local copies, waits for them, and re-layouts: 1.74 us -> 0 us
  Pallas kernels: 33.4 us -> 32.1 us
    pallas_call x1, Pallas kernels: 33.4 us -> 30.9 us  [on_device(): pl.pallas_call(kernel, name='outer_step', out_shape=(pltpu.VMEM((rows, co...]
    unnamed x2 -> x0, local copies, waits for them, and re-layouts: 1.74 us -> none
    pallas_call x0 -> x1, Pallas kernels: none -> 1.13 us  [on_device(): pl.pallas_call(store, name='store', out_shape=tuple((pltpu.HBM(array.shap...]
where the time goes in v5:
time: 32.8 us; the launch traced here: 32.7 us
  Pallas kernels  32.1 us (98%)
  between operations  0.64 us (2%)
    pallas_call x1, Pallas kernels, on_device(): pl.pallas_call(kernel, name='outer_step', out_shape=(pltpu.VMEM((rows, co...  30.9 us
    pallas_call x1, Pallas kernels, on_device(): pl.pallas_call(store, name='store', out_shape=tuple((pltpu.HBM(array.shap...  1.13 us

profile of v5, /device:TPU:1, one launch (start us, length us, event | category | flops | bytes accessed | tf_op | source)
XLA Modules:
  0.0 32.7 jit_solution(13275340118743278501)
XLA Ops:
  0.6 30.9 %outer_step.1 = (bf16[256,2816]{1,0:T(8,128)(2,1)S(1)}, f32[8,2816]{1,0:T(8,128)S(1)}) custom-call(bf16[1,256,2816]{2,1,0:T(8,128)(2,1)} %params.1, bf16[256,2816]{1,0:T(8,128)(2,1)} %base.1, f32[8,2816]{1,0:T(8,128)} %momentum.1, s32[2,22]{1,0:T(2,128)} %enc_exp.1, s32[2,22]{1,0:T(2,128)} %ret_exp.1), custom_call_target="tpu_custom_call" | custom-call | flops 20000000 | bytes 4500000 | tf_op jit(solution)/shard_map/outer_step/pallas_call | solution.py:413
  31.6 1.1 %store.1 = (bf16[256,2816]{1,0:T(8,128)(2,1)}, f32[8,2816]{1,0:T(8,128)}) custom-call(bf16[256,2816]{1,0:T(8,128)(2,1)S(1)} %get-tuple-element.4.params, f32[8,2816]{1,0:T(8,128)S(1)} %get-tuple-element.5.momentum), custom_call_target="tpu_custom_call" | custom-call | tf_op jit(solution)/shard_map/store/pallas_call | solution.py:446

commit v6 on v5

--- a/solution.py
+++ b/solution.py
@@ -15,22 +15,22 @@
 ZROWS = 16
 XROWS = NZ * ZROWS
 
-ONE, ZFIRST = range(2)
-CHUNKS = ((0, 2, ONE), (2, 5, ONE), (5, 8, ONE), (8, 10, ZFIRST), (10, 11, ZFIRST))
-BLOCKS, EXPONENTS, OTHER_BASE = 0, 5, 6
-LOADS = 7
-SWAP, SHARDS, SUMS, CODES, GATHER, CORE, MOMENT = range(7)
-SENDS = 7
+ONE, ZFIRST, BOTH = range(3)
+CHUNKS = ((0, 3, ONE), (3, 6, ONE), (6, 8, BOTH), (8, 9, ZFIRST), (9, 11, ZFIRST))
+EXPONENTS, OTHER_BASE = range(2)
+LOADS = 2
+SWAP, SHARDS, SUMS, CODES, GATHER, CORE, MOMENT, TWICE = range(8)
+SENDS = 8
 IN_SWAP, IN_MOMENT, IN_MOMENT_BACK, IN_CHUNKS = 0, 5, 6, 7
 Z_TILE = min([lo for lo, _, how in CHUNKS if how == ZFIRST], default=0)
 WHOLE = 4
-FIRST, OWNED, SECOND, FAR_IN, CORE_FAR, CODES_IN, NEAR_IN, CORE_NEAR = 0, 1, 2, 3, 4, 5, 9, 10
+FIRST, SECOND, FAR_IN, CORE_FAR, CODES_IN, NEAR_IN, CORE_NEAR = 0, 1, 2, 3, 4, 8, 9
 
 
 def chunk_starts():
     starts = [IN_CHUNKS]
     for _, _, how in CHUNKS:
-        starts.append(starts[-1] + (9 if how == ZFIRST else 11))
+        starts.append(starts[-1] + (8 if how == ZFIRST else 10))
     return starts
 
 
@@ -42,13 +42,13 @@
 SCHEDULE = (
     (ENCODE, 0), (ENCODE, 1), (ENCODE, 2), (PAIR, 0), (PAIR, 1), (PAIR, 2),
     (ENCODE, 3), (ENCODE, 4), (SEND_OWNED, 0), (SEND_OWNED, 1), (SEND_OWNED, 2), (SEND_OWNED, 3),
-    (SEND_OWNED, 4), (SUM, 0), (SUM, 1), (SUM, 3), (SUM, 2), (SUM, 4),
-    (STEP, 0), (STEP, 1), (STEP, 3), (STEP, 4), (STEP, 2), (RING, 0),
-    (OWN, 0), (RING, 3), (RING, 4), (RING, 1), (OWN, 1), (RING, 2),
-    (OWN, 2), (LAND_NEAR, 0), (OWN_NEAR, 0), (LAND, 0), (OWN_FAR, 0), (OTHER_NEAR, 0),
-    (OTHER_FAR, 0), (LAND_NEAR, 1), (LAND, 1), (OWN_NEAR, 1), (OWN_FAR, 1), (LAND, 3),
-    (OWN_FAR, 3), (OTHER_NEAR, 1), (OTHER_FAR, 1), (LAND_NEAR, 2), (LAND, 2), (OWN_NEAR, 2),
-    (LAND, 4), (OWN_FAR, 2), (OWN_FAR, 4), (OTHER_FAR, 3), (OTHER_NEAR, 2), (OTHER_FAR, 2),
+    (SEND_OWNED, 4), (SUM, 0), (SUM, 3), (SUM, 1), (SUM, 2), (SUM, 4),
+    (STEP, 3), (STEP, 0), (STEP, 1), (STEP, 4), (STEP, 2), (RING, 3),
+    (RING, 0), (OWN, 0), (RING, 4), (RING, 1), (OWN, 1), (RING, 2),
+    (OWN, 2), (LAND, 3), (OWN_FAR, 3), (OTHER_NEAR, 2), (LAND_NEAR, 0), (LAND, 0),
+    (OWN_NEAR, 0), (OWN_FAR, 0), (OTHER_FAR, 3), (OTHER_NEAR, 0), (OTHER_FAR, 0), (LAND_NEAR, 1),
+    (LAND, 1), (OWN_NEAR, 1), (OWN_FAR, 1), (LAND, 4), (OWN_FAR, 4), (OTHER_NEAR, 1),
+    (OTHER_FAR, 1), (LAND, 2), (OTHER_FAR, 2), (OWN_FAR, 2), (LAND_NEAR, 2), (OWN_NEAR, 2),
     (OTHER_FAR, 4),
 )
 
@@ -65,13 +65,13 @@
 
 def kernel(
     params, base, momentum, enc_exp, ret_exp, new_params, new_momentum,
-    exp_words, mine, sib_params, oth_base, exps, enc_mul, enc_scale, ret_mul, ret_scale,
+    exp_words, mine, oth_base, exps, enc_mul, enc_scale, ret_mul, ret_scale,
     shards, x_in, z_in, t_wide, t_narrow, moment, moment_out, codes, sib_codes,
     load_sem, send_sem, recv_sem,
 ):
     rep = lax.axis_index("rep")
     x, z, c = rep // (NZ * 2), (rep // 2) % NZ, rep % 2
-    width = sib_params.shape[1]
+    width = mine.shape[2]
     tiles = width // BLOCK
 
     def place(px, pz, pc):
@@ -81,6 +81,7 @@
     right, far, left = (x + 1) % NX, (x + 2) % NX, (x + 3) % NX
     x_devs = [place((x + d) % NX, z, c) for d in (1, 2, 3)]
     z_devs = [place(x, (z + d) % NZ, c) for d in (1, 2, 3)]
+    cross_devs = [place((x + d) % NX, z, 1 - c) for d in (1, 2, 3)]
 
     def rows_of(block):
         return pl.ds(pl.multiple_of(block * XROWS, XROWS), XROWS)
@@ -90,6 +91,9 @@
 
     def local(src, dst, sem):
         pltpu.make_async_copy(src, dst, load_sem.at[sem]).start()
+
+    def beside_swap(src, dst, arrival):
+        pltpu.make_async_copy(src, dst, recv_sem.at[arrival]).start()
 
     def remote(src, dst, device, send, arrival):
         pltpu.make_async_remote_copy(
@@ -110,7 +114,7 @@
         take(send_sem.at[sem], ref)
 
     barrier = pltpu.get_barrier_semaphore()
-    for device in x_devs + z_devs + [sibling]:
+    for device in x_devs + z_devs + cross_devs + [sibling]:
         pl.semaphore_signal(barrier, inc=1, device_id=device, device_id_type=MESH)
 
     order = (far, right, left, x)
@@ -128,23 +132,23 @@
     for which in pieces:
         rows, first, count = piece(which)
         lanes = pl.ds(first, count)
-        local(base.at[rows, columns(c, first, count)], mine.at[0, rows, lanes], BLOCKS + which)
-        local(params.at[0, rows, columns(c, first, count)], mine.at[1, rows, lanes], BLOCKS + which)
+        beside_swap(base.at[rows, columns(c, first, count)], mine.at[0, rows, lanes], IN_SWAP + which)
+        beside_swap(params.at[0, rows, columns(c, first, count)], mine.at[1, rows, lanes], IN_SWAP + which)
     local(enc_exp, exp_words.at[0], EXPONENTS)
     local(ret_exp, exp_words.at[1], EXPONENTS)
 
-    pl.semaphore_wait(barrier, 7)
+    pl.semaphore_wait(barrier, 10)
 
     for which in pieces:
         rows, first, count = piece(which)
         remote(
-            params.at[0, rows, columns(1 - c, first, count)], sib_params.at[rows, pl.ds(first, count)],
+            params.at[0, rows, columns(1 - c, first, count)], mine.at[2, rows, pl.ds(first, count)],
             sibling, SWAP, IN_SWAP + which,
         )
     moment_rows = pl.ds(pl.multiple_of(c * 8, 8), 8)
     other_rows = pl.ds(pl.multiple_of((1 - c) * 8, 8), 8)
     remote(momentum.at[:, oth_cols], moment.at[moment_rows], sibling, MOMENT, IN_MOMENT)
-    pltpu.make_async_copy(momentum.at[:, own_cols], moment.at[moment_rows], recv_sem.at[IN_MOMENT]).start()
+    beside_swap(momentum.at[:, own_cols], moment.at[moment_rows], IN_MOMENT)
     local(base.at[:, oth_cols], oth_base, OTHER_BASE)
 
     loaded(EXPONENTS, exp_words)
@@ -176,8 +180,7 @@
                 ready.add(which)
                 rows, first, count = piece(which)
                 lanes = pl.ds(first, count)
-                loaded(BLOCKS + which, mine.at[:, rows, lanes])
-                arrived(IN_SWAP + which, sib_params.at[rows, lanes])
+                arrived(IN_SWAP + which, mine.at[:, rows, lanes])
 
     def encoded_pair(which, tile):
         block = order[which]
@@ -186,7 +189,7 @@
         factor = enc_mul[pl.ds((block // 2) * tiles + tile, 1), :]
         start = mine[0, rows, lanes].astype(F32)
         total = None
-        for source in (mine[1, rows, lanes], sib_params[rows, lanes]):
+        for source in (mine[1, rows, lanes], mine[2, rows, lanes]):
             code = jnp.clip((source.astype(F32) - start) * factor, -CODE_LIMIT, CODE_LIMIT)
             code = code.astype(BF16).astype(F32)
             total = code if total is None else total + code
@@ -211,7 +214,7 @@
             shards[tile, order[which]] = encoded_pair(which, tile).astype(BF16)
 
     def encode(k):
-        if mode(k) == ONE:
+        if mode(k) != ZFIRST:
             need(0, 1, 2)
             for which, d in ((0, 2), (1, 1), (2, 3)):
                 fill(which, k)
@@ -235,15 +238,15 @@
 
     def send_owned(k):
         for d in (2, 1, 3):
-            if mode(k) == ONE:
+            if mode(k) != ZFIRST:
                 remote(
                     shards.at[part(k), (x + d) % NX, z], x_in.at[d - 1, part(k), z], x_devs[d - 1],
-                    SHARDS, event(k, OWNED),
+                    SHARDS, event(k, SECOND),
                 )
             else:
                 remote(
                     shards.at[part(k), x, (z + d) % NZ], z_in.at[d - 1, part(k), x], z_devs[d - 1],
-                    SHARDS, event(k, OWNED),
+                    SHARDS, event(k, SECOND),
                 )
 
     def pair(k):
@@ -252,7 +255,7 @@
             t_wide[tile] = encoded_pair(3, tile)
 
     def first_total(k, tile, at):
-        if mode(k) == ONE:
+        if mode(k) != ZFIRST:
             total, parts = t_wide[tile, at], x_in
         else:
             total, parts = shards[tile, at, z].astype(F32), z_in
@@ -261,25 +264,24 @@
         return total
 
     def sum_first(k):
-        arrived(event(k, FIRST), (x_in if mode(k) == ONE else z_in).at[:, part(k), pl.ds(0, 3)])
+        arrived(event(k, FIRST), (x_in if mode(k) != ZFIRST else z_in).at[:, part(k), pl.ds(0, 3)])
         for d in (2, 1, 3):
-            at = ((z if mode(k) == ONE else x) + d) % NZ
+            at = ((z if mode(k) != ZFIRST else x) + d) % NZ
             for tile in span(k):
                 t_narrow[tile, at] = first_total(k, tile, at).astype(BF16)
-            landing, devices = (z_in, z_devs) if mode(k) == ONE else (x_in, x_devs)
+            landing, devices = (z_in, z_devs) if mode(k) != ZFIRST else (x_in, x_devs)
             remote(t_narrow.at[part(k), at], landing.at[d - 1, part(k), 0], devices[d - 1], SUMS, event(k, SECOND))
 
     started = set()
 
     def step(k):
         return_tables()
-        if not started:
-            started.add(True)
+        if IN_MOMENT not in started:
+            started.add(IN_MOMENT)
             arrived(IN_MOMENT, moment)
         second = x_in if mode(k) == ZFIRST else z_in
         mine_at = x if mode(k) == ZFIRST else z
-        arrived(event(k, OWNED), second.at[:, part(k), 0])
-        arrived(event(k, SECOND), second.at[:, part(k), 0])
+        arrived(event(k, SECOND), shards.at[part(k), pl.ds(0, 2), pl.ds(0, 3)])
         for tile in span(k):
             lanes = slice(tile * BLOCK, (tile + 1) * BLOCK)
             at = pl.ds((x // 2) * tiles + tile, 1)
@@ -294,36 +296,39 @@
             codes[tile, x, z] = code.astype(BF16)
         piece = codes.at[part(k), x, z]
         for d in (2, 1, 3):
-            if mode(k) == ONE:
+            if mode(k) != ZFIRST:
                 remote(piece, piece, z_devs[d - 1], CODES, event(k, CODES_IN + z))
             else:
                 remote(piece, piece, x_devs[d - 1], CODES, event(k, CODES_IN + x))
-        gather(k, piece)
-
-    def gather(k, piece):
+        gather(k, piece, z if mode(k) != ZFIRST else x)
+
+    def gather(k, piece, at):
         for d in (2, 1, 3):
-            if mode(k) == ONE:
+            if mode(k) != ZFIRST:
                 remote(piece, piece, x_devs[d - 1], GATHER, event(k, FAR_IN if d == 2 else NEAR_IN))
             else:
                 remote(piece, piece, z_devs[d - 1], GATHER, event(k, FAR_IN))
+            if mode(k) == BOTH:
+                remote(piece, sib_codes.at[part(k), x, at], cross_devs[d - 1], TWICE, event(k, CORE_FAR))
 
     def to_sibling(k, block, arrival):
-        remote(codes.at[part(k), block], sib_codes.at[part(k), block], sibling, CORE, event(k, arrival))
+        remote(codes.at[part(k), block], sib_codes.at[part(k), block], sibling, TWICE if mode(k) == BOTH else CORE, event(k, arrival))
 
     line_order = [jnp.where(z < 2, at, 3 - at) for at in (1 - jnp.minimum(z, 3 - z), 2, 3)]
 
     def ring(k):
-        for at in line_order if mode(k) == ONE else (right, left, far):
-            piece = codes.at[part(k), x, at] if mode(k) == ONE else codes.at[part(k), at, z]
+        for at in line_order if mode(k) != ZFIRST else (right, left, far):
+            piece = codes.at[part(k), x, at] if mode(k) != ZFIRST else codes.at[part(k), at, z]
             arrived(event(k, CODES_IN + at), piece)
-            gather(k, piece)
-        if mode(k) == ONE:
+            gather(k, piece, at)
+        if mode(k) != ZFIRST:
             to_sibling(k, x, CORE_NEAR)
 
     def land_near(k):
         arrived(event(k, NEAR_IN), codes.at[part(k), pl.ds(0, 2)])
-        to_sibling(k, right, CORE_NEAR)
-        to_sibling(k, left, CORE_NEAR)
+        if mode(k) != BOTH:
+            to_sibling(k, right, CORE_NEAR)
+            to_sibling(k, left, CORE_NEAR)
 
     def land(k):
         if mode(k) == ZFIRST:
@@ -331,7 +336,8 @@
             remote(codes.at[part(k)], sib_codes.at[part(k)], sibling, CORE, event(k, CORE_FAR))
         else:
             arrived(event(k, FAR_IN), codes.at[part(k), 0])
-            to_sibling(k, far, CORE_FAR)
+            if mode(k) != BOTH:
+                to_sibling(k, far, CORE_FAR)
 
     def apply(k, block, own):
         rows = rows_of(block)
@@ -358,13 +364,15 @@
             apply(k, block, True)
 
     def other_near(k):
-        arrived(event(k, CORE_NEAR), codes.at[part(k), pl.ds(0, 3)])
-        for block in (x, right, left):
+        blocks = (x,) if mode(k) == BOTH else (x, right, left)
+        arrived(event(k, CORE_NEAR), codes.at[part(k), pl.ds(0, len(blocks))])
+        for block in blocks:
             apply(k, block, False)
 
     def other_far(k):
-        arrived(event(k, CORE_FAR), codes.at[part(k)] if mode(k) == ZFIRST else codes.at[part(k), 0])
-        for block in order if mode(k) == ZFIRST else (far,):
+        blocks = {ONE: (far,), ZFIRST: order, BOTH: (far, right, left)}[mode(k)]
+        arrived(event(k, CORE_FAR), codes.at[part(k), pl.ds(0, len(blocks))])
+        for block in blocks:
             apply(k, block, False)
 
     stages = {
@@ -383,12 +391,15 @@
                 new_momentum[:, own_cols] = moment_out[moment_rows]
     arrived(IN_MOMENT_BACK, new_momentum.at[:, oth_cols])
 
-    sent(SWAP, sib_params)
+    sent(SWAP, mine.at[2])
     sent(SHARDS, shards.at[:, pl.ds(0, 3)])
     sent(SUMS, t_narrow.at[:, pl.ds(0, 3)])
     sent(CODES, t_narrow.at[:, pl.ds(0, 3)])
     sent(GATHER, codes.at[:, pl.ds(0, 3)])
-    sent(CORE, codes)
+    twice = sum(hi - lo for lo, hi, how in CHUNKS if how == BOTH)
+    sent(CORE, codes.at[pl.ds(0, tiles - twice)])
+    if twice:
+        sent(TWICE, codes.at[pl.ds(0, twice)])
     sent(MOMENT, moment)
 
 
@@ -407,7 +418,6 @@
     width = columns // 2
     tiles = width // BLOCK
     table = pltpu.VMEM((-(-4 * tiles // 8) * 8, BLOCK), F32)
-    half = pltpu.VMEM((rows, width), BF16)
     hbm = pl.BlockSpec(memory_space=pltpu.HBM)
     vmem = pl.BlockSpec(memory_space=pltpu.VMEM)
     held = pl.pallas_call(
@@ -418,8 +428,8 @@
         out_specs=(vmem, vmem),
         scratch_shapes=[
             pltpu.SMEM((2,) + encode_exponents.shape, jnp.int32),
-            pltpu.VMEM((2, rows, width), BF16),
-            half, half,
+            pltpu.VMEM((3, rows, width), BF16),
+            pltpu.VMEM((rows, width), BF16),
             pltpu.VMEM((2, -(-4 * tiles // 8) * 8, BLOCK), jnp.int32),
             table, table, table, table,
             pltpu.VMEM((tiles, NX, NZ, ZROWS, BLOCK), BF16),

time: 32.8 us -> 32.8 us (level)
  no operation moved by 1% of the time
where the time goes in v6:
time: 32.8 us; the launch traced here: 32.7 us
  Pallas kernels  32 us (98%)
  between operations  0.64 us (2%)
    pallas_call x1, Pallas kernels, on_device(): pl.pallas_call(kernel, name='outer_step', out_shape=(pltpu.VMEM((rows, co...  30.9 us
    pallas_call x1, Pallas kernels, on_device(): pl.pallas_call(store, name='store', out_shape=tuple((pltpu.HBM(array.shap...  1.13 us

profile of v6, /device:TPU:1, one launch (start us, length us, event | category | flops | bytes accessed | tf_op | source)
XLA Modules:
  0.0 32.7 jit_solution(2213153221097870633)
XLA Ops:
  0.6 30.9 %outer_step.1 = (bf16[256,2816]{1,0:T(8,128)(2,1)S(1)}, f32[8,2816]{1,0:T(8,128)S(1)}) custom-call(bf16[1,256,2816]{2,1,0:T(8,128)(2,1)} %params.1, bf16[256,2816]{1,0:T(8,128)(2,1)} %base.1, f32[8,2816]{1,0:T(8,128)} %momentum.1, s32[2,22]{1,0:T(2,128)} %enc_exp.1, s32[2,22]{1,0:T(2,128)} %ret_exp.1), custom_call_target="tpu_custom_call" | custom-call | flops 20000000 | bytes 4500000 | tf_op jit(solution)/shard_map/outer_step/pallas_call | solution.py:423
  31.6 1.1 %store.1 = (bf16[256,2816]{1,0:T(8,128)(2,1)}, f32[8,2816]{1,0:T(8,128)}) custom-call(bf16[256,2816]{1,0:T(8,128)(2,1)S(1)} %get-tuple-element.4.params, f32[8,2816]{1,0:T(8,128)S(1)} %get-tuple-element.5.momentum), custom_call_target="tpu_custom_call" | custom-call | tf_op jit(solution)/shard_map/store/pallas_call | solution.py:456

commit v7 on v6

--- a/solution.py
+++ b/solution.py
@@ -129,6 +129,14 @@
         return pl.ds(pl.multiple_of(core * width + first, BLOCK), count)
 
     pieces = (0, 1, 2, 3, WHOLE)
+    pl.semaphore_wait(barrier, 10)
+
+    for which in pieces:
+        rows, first, count = piece(which)
+        remote(
+            params.at[0, rows, columns(1 - c, first, count)], mine.at[2, rows, pl.ds(first, count)],
+            sibling, SWAP, IN_SWAP + which,
+        )
     for which in pieces:
         rows, first, count = piece(which)
         lanes = pl.ds(first, count)
@@ -137,14 +145,6 @@
     local(enc_exp, exp_words.at[0], EXPONENTS)
     local(ret_exp, exp_words.at[1], EXPONENTS)
 
-    pl.semaphore_wait(barrier, 10)
-
-    for which in pieces:
-        rows, first, count = piece(which)
-        remote(
-            params.at[0, rows, columns(1 - c, first, count)], mine.at[2, rows, pl.ds(first, count)],
-            sibling, SWAP, IN_SWAP + which,
-        )
     moment_rows = pl.ds(pl.multiple_of(c * 8, 8), 8)
     other_rows = pl.ds(pl.multiple_of((1 - c) * 8, 8), 8)
     remote(momentum.at[:, oth_cols], moment.at[moment_rows], sibling, MOMENT, IN_MOMENT)

time: 32.8 us -> 32.8 us (level)
  no operation moved by 1% of the time
where the time goes in v7:
time: 32.8 us; the launch traced here: 32.6 us
  Pallas kernels  32 us (98%)
  between operations  0.64 us (2%)
    pallas_call x1, Pallas kernels, on_device(): pl.pallas_call(kernel, name='outer_step', out_shape=(pltpu.VMEM((rows, co...  30.9 us
    pallas_call x1, Pallas kernels, on_device(): pl.pallas_call(store, name='store', out_shape=tuple((pltpu.HBM(array.shap...  1.13 us

profile of v7, /device:TPU:1, one launch (start us, length us, event | category | flops | bytes accessed | tf_op | source)
XLA Modules:
  0.0 32.6 jit_solution(6738304567733683469)
XLA Ops:
  0.6 30.9 %outer_step.1 = (bf16[256,2816]{1,0:T(8,128)(2,1)S(1)}, f32[8,2816]{1,0:T(8,128)S(1)}) custom-call(bf16[1,256,2816]{2,1,0:T(8,128)(2,1)} %params.1, bf16[256,2816]{1,0:T(8,128)(2,1)} %base.1, f32[8,2816]{1,0:T(8,128)} %momentum.1, s32[2,22]{1,0:T(2,128)} %enc_exp.1, s32[2,22]{1,0:T(2,128)} %ret_exp.1), custom_call_target="tpu_custom_call" | custom-call | flops 20000000 | bytes 4500000 | tf_op jit(solution)/shard_map/outer_step/pallas_call | solution.py:423
  31.5 1.1 %store.1 = (bf16[256,2816]{1,0:T(8,128)(2,1)}, f32[8,2816]{1,0:T(8,128)}) custom-call(bf16[256,2816]{1,0:T(8,128)(2,1)S(1)} %get-tuple-element.4.params, f32[8,2816]{1,0:T(8,128)S(1)} %get-tuple-element.5.momentum), custom_call_target="tpu_custom_call" | custom-call | tf_op jit(solution)/shard_map/store/pallas_call | solution.py:456
